TPU v7x, 32 devices: a whole 2x2x4 slice. The times are simulated.
32 devices in a mesh: basin: 4 (over y, x), blk: 8 (over z, core).
Axes of the slice: x: 2, y: 2, z: 4, core: 2. Of those that a mesh axis runs over, the one named last changes fastest.
Arguments:
- terminal: float32 [64, 128, 128], P(('basin', 'blk')), may hold values from -6 to 6
- depth: float32 [64, 128, 128], P(('basin', 'blk')), may hold values from 1.5 to 4.5
- wet_cells: int32 [64, 128, 128], P(('basin', 'blk')), may hold values from 0 to 1
- neighbours: int32 [64, 4], P(('basin', 'blk')), may hold values from -1 to 63, as said below
- gauge_cell: int32 [1024], P(('basin', 'blk')), may hold values from 0 to 32767
- misfit: float32 [4, 1024], P(None, ('basin', 'blk')), may hold values from -6 to 6
- basis: float32 [64, 4, 128, 128], P(('basin', 'blk')), may hold values from -0.046875 to 0.046875
- subfault_index: int32 [64, 4], P(('basin', 'blk')), may hold values from 0 to 255, as said below
- source: float32 [256], P(('basin', 'blk')), may hold values from -6 to 6
- background: float32 [256], P(('basin', 'blk')), may hold values from -6 to 6
- step_size: float32 [1], replicated, may hold values from 0.25 to 1
Outputs:
- surface: float32 [64, 128, 128], P(('basin', 'blk'))
- updated: float32 [256], P(('basin', 'blk'))
Inputs may be any that keep to these rules, and one draw needn't show every extreme that they name: `neighbours`: entry (s, side) is the global slot (device index along basin+blk times 2 plus slot) of the wet block beside slot s's block on the west, east, south or north side, or -1 where that block is dry or off the grid. The relation is mutual: if slot a names b on the west, b names a on the east, and likewise south and north. A named slot lies on a device of the same basin index or of the basin index one lower or higher, wrapping around. Of one device's rows, at most 2 entries name slots of any one other device, and some pair of devices reaches 2. `subfault_index`: A subfault's deformation spans several blocks: every subfault that is named at all is named by two or more entries, in one slot's row or in several.
All inputs are finite; a program needn't handle non-finite values.
Results may differ from a plain program's by a relative error of at most 0.000059.
Values sent between devices are 32-bit elements; how exact they have to be, the bound alone decides.
A program may use at most 64 MiB of HBM per device.

v0:
```python
import jax
import jax.numpy as jnp
from jax import lax
from jax.sharding import PartitionSpec as P

coupling = 0.5
prior_weight = 0.5


def with_halo(block, sides, width):
    for axis, dim in sides:
        count = lax.axis_size(axis)
        forward = [(i, i + 1) for i in range(count - 1)]
        forward.append((count - 1, 0))
        backward = [(target, source) for source, target in forward]
        low = lax.ppermute(
            lax.slice_in_dim(block, block.shape[dim] - width, None, axis=dim), axis, forward
        )
        high = lax.ppermute(lax.slice_in_dim(block, 0, width, axis=dim), axis, backward)
        block = jnp.concatenate([low, block, high], axis=dim)
    return block


def along_x(field, west, east):
    ahead = jnp.concatenate([field[:, :, 1:], east[:, :, None]], axis=2)
    behind = jnp.concatenate([west[:, :, None], field[:, :, :-1]], axis=2)
    return 0.5 * (ahead - behind)


def along_y(field, south, north):
    ahead = jnp.concatenate([field[:, 1:, :], north[:, None, :]], axis=1)
    behind = jnp.concatenate([south[:, None, :], field[:, :-1, :]], axis=1)
    return 0.5 * (ahead - behind)


def edge_rows(first, second):
    stacked = jnp.stack(
        [first[:, :, 0], first[:, :, -1], second[:, 0, :], second[:, -1, :]], axis=1
    )
    return stacked.reshape(-1, first.shape[2])


def shards(
    terminal,
    depth,
    wet_cells,
    neighbours,
    gauge_cell,
    misfit,
    basis,
    subfault_index,
    source,
    background,
    step_size,
):
    slot_count, block_side, _ = terminal.shape
    edge_count = slot_count * 4
    basin_count = lax.axis_size("basin")
    group_count = lax.axis_size("blk")
    basin_index = lax.axis_index("basin")
    group_index = lax.axis_index("blk")
    own_device = basin_index * group_count + group_index
    present = (neighbours >= 0).reshape(-1)
    safe_index = jnp.where(present, neighbours.reshape(-1), 0)
    owner_device = safe_index // slot_count
    sides = jnp.tile(jnp.arange(4, dtype=jnp.int32), slot_count)
    opposite = sides + 1 - 2 * (sides % 2)
    source_edge = safe_index % slot_count * 4 + opposite
    owner_group = owner_device % group_count
    heading = (owner_device // group_count - basin_index + 1) % basin_count
    remote = present & (owner_device != own_device)
    peer_key = heading * group_count + owner_group
    same_peer = (peer_key[:, None] == peer_key[None, :]) & remote[None, :]
    positions = jnp.arange(edge_count)
    send_rank = jnp.sum(same_peer & (positions[None, :] < positions[:, None]), axis=1)
    recv_rank = jnp.sum(same_peer & (source_edge[None, :] < source_edge[:, None]), axis=1)
    spare_row = group_count * 3 * slot_count
    target = jnp.where(remote, (owner_group * 3 + heading) * slot_count + send_rank, spare_row)
    lookup = jnp.where(
        remote, heading * (group_count * slot_count) + owner_group * slot_count + recv_rank, 0
    )

    def collect(packed):
        outgoing = jnp.zeros((spare_row + 1, block_side), packed.dtype).at[target].set(packed)
        outgoing = outgoing[:-1].reshape(group_count, 3, slot_count, block_side)
        arrived = lax.all_to_all(outgoing, "blk", split_axis=0, concat_axis=0, tiled=True)
        crossing = jnp.stack([arrived[:, 0], arrived[:, 2]], axis=0)
        beside_all = with_halo(crossing, (("basin", 0),), 1)
        edge_table = jnp.stack([beside_all[0], arrived[:, 1], beside_all[3]], axis=0).reshape(
            -1, block_side
        )
        fetched = jnp.where(remote[:, None], edge_table[lookup], packed[source_edge])
        return jnp.where(present[:, None], fetched, 0.0).reshape(slot_count, 4, block_side)

    wet_float = wet_cells.astype(jnp.float32)
    surface = terminal
    east_flow = jnp.zeros_like(terminal)
    north_flow = jnp.zeros_like(terminal)
    for moment in range(misfit.shape[0]):
        forcing = surface.reshape(-1).at[gauge_cell].add(misfit[moment]).reshape(surface.shape)
        masked = wet_float * forcing
        rims = collect(edge_rows(masked, masked))
        east_flow = wet_float * (
            east_flow + coupling * depth * along_x(masked, rims[:, 0], rims[:, 1])
        )
        north_flow = wet_float * (
            north_flow + coupling * depth * along_y(masked, rims[:, 2], rims[:, 3])
        )
        rims = collect(edge_rows(east_flow, north_flow))
        surface = masked + coupling * (
            along_x(east_flow, rims[:, 0], rims[:, 1]) + along_y(north_flow, rims[:, 2], rims[:, 3])
        )
    partial_value = jnp.einsum("sjyx,syx->sj", basis, surface, precision=lax.Precision.HIGHEST)
    owned = source.shape[0]
    total_count = owned * basin_count * group_count
    spread = (
        jnp.zeros((total_count,), jnp.float32)
        .at[subfault_index.reshape(-1)]
        .add(partial_value.reshape(-1))
    )
    whole = lax.psum(spread, ("basin", "blk"))
    mine = lax.dynamic_slice_in_dim(whole, own_device * owned, owned)
    gradient = prior_weight * (source - background) + mine
    return (surface, source - step_size[0] * gradient)


def solution(mesh):
    in_specs = (
        P(("basin", "blk"), None, None),
        P(("basin", "blk"), None, None),
        P(("basin", "blk"), None, None),
        P(("basin", "blk"), None),
        P(("basin", "blk")),
        P(None, ("basin", "blk")),
        P(("basin", "blk"), None, None, None),
        P(("basin", "blk"), None),
        P(("basin", "blk")),
        P(("basin", "blk")),
        P(),
    )
    out_specs = (P(("basin", "blk"), None, None), P(("basin", "blk")))
    return jax.shard_map(shards, mesh=mesh, in_specs=in_specs, out_specs=out_specs, check_vma=False)
```

profile of v0, /device:TPU:0, one launch (start us, length us, event | category | flops | bytes accessed | tf_op | source)
XLA Modules:
  0.0 188.9 jit_solution(14475373771681279796)
XLA Ops:
  5.9 6.3 %all-to-all-start = ((f32[8,3,2,128]{3,2,1,0:T(2,128)}), f32[8,3,2,128]{3,2,1,0:T(2,128)S(1)}, u32[]{:S(2)}, u32[]{:S(2)}) async-start(f32[8,3,2,128]{3,2,1,0:T(2,128)} %bitcast.10), calls=%async_computation | async-start | bytes 49152 | tf_op jit(solution)/shard_map/all_to_all | solution.py:86
  13.1 4.8 %all-to-all-done = f32[8,3,2,128]{3,2,1,0:T(2,128)S(1)} async-done(((f32[8,3,2,128]{3,2,1,0:T(2,128)}), f32[8,3,2,128]{3,2,1,0:T(2,128)S(1)}, u32[]{:S(2)}, u32[]{:S(2)}) %all-to-all-start) | async-done | bytes 24608 | tf_op jit(solution)/shard_map/all_to_all | solution.py:86
  17.9 1.5 collective-permute-start
  19.4 1.4 collective-permute-start.1
  26.3 3.3 %all-to-all-start.1 = ((f32[8,3,2,128]{3,2,1,0:T(2,128)}), f32[8,3,2,128]{3,2,1,0:T(2,128)S(1)}, u32[]{:S(2)}, u32[]{:S(2)}) async-start(f32[8,3,2,128]{3,2,1,0:T(2,128)} %bitcast.25), calls=%async_computation.1 | async-start | bytes 49152 | tf_op jit(solution)/shard_map/all_to_all | solution.py:86
  29.7 5.6 %all-to-all-done.1 = f32[8,3,2,128]{3,2,1,0:T(2,128)S(1)} async-done(((f32[8,3,2,128]{3,2,1,0:T(2,128)}), f32[8,3,2,128]{3,2,1,0:T(2,128)S(1)}, u32[]{:S(2)}, u32[]{:S(2)}) %all-to-all-start.1) | async-done | bytes 24608 | tf_op jit(solution)/shard_map/all_to_all | solution.py:86
  35.3 2.4 %collective-permute-start.2 = (f32[1,8,2,128]{3,2,1,0:T(2,128)S(1)}, f32[1,8,2,128]{3,2,1,0:T(2,128)S(1)}, u32[]{:S(2)}, u32[]{:S(2)}) collective-permute-start(f32[1,8,2,128]{3,2,1,0:T(2,128)S(1)} %get-tuple-element.101), channel_id=1, source_target_pairs={{0,8},{8,16},{16,24},{24,0},{1,9},{9,17},{17,25},{25,1},{2,10},{10... | collective-permute-start | bytes 24584 | tf_op jit(solution)/shard_map/ppermute | solution.py:16
  39.9 1.5 collective-permute-done.3
  44.9 3.3 %all-to-all-start.2 = ((f32[8,3,2,128]{3,2,1,0:T(2,128)}), f32[8,3,2,128]{3,2,1,0:T(2,128)S(1)}, u32[]{:S(2)}, u32[]{:S(2)}) async-start(f32[8,3,2,128]{3,2,1,0:T(2,128)} %bitcast.40), calls=%async_computation.2 | async-start | bytes 49152 | tf_op jit(solution)/shard_map/all_to_all | solution.py:86
  48.3 5.5 %all-to-all-done.2 = f32[8,3,2,128]{3,2,1,0:T(2,128)S(1)} async-done(((f32[8,3,2,128]{3,2,1,0:T(2,128)}), f32[8,3,2,128]{3,2,1,0:T(2,128)S(1)}, u32[]{:S(2)}, u32[]{:S(2)}) %all-to-all-start.2) | async-done | bytes 24608 | tf_op jit(solution)/shard_map/all_to_all | solution.py:86
  53.9 1.5 collective-permute-start.4
  55.4 1.4 collective-permute-start.5
  61.7 3.3 %all-to-all-start.3 = ((f32[8,3,2,128]{3,2,1,0:T(2,128)}), f32[8,3,2,128]{3,2,1,0:T(2,128)S(1)}, u32[]{:S(2)}, u32[]{:S(2)}) async-start(f32[8,3,2,128]{3,2,1,0:T(2,128)} %bitcast.52), calls=%async_computation.3 | async-start | bytes 49152 | tf_op jit(solution)/shard_map/all_to_all | solution.py:86
  65.0 5.6 %all-to-all-done.3 = f32[8,3,2,128]{3,2,1,0:T(2,128)S(1)} async-done(((f32[8,3,2,128]{3,2,1,0:T(2,128)}), f32[8,3,2,128]{3,2,1,0:T(2,128)S(1)}, u32[]{:S(2)}, u32[]{:S(2)}) %all-to-all-start.3) | async-done | bytes 24608 | tf_op jit(solution)/shard_map/all_to_all | solution.py:86
  70.7 1.4 collective-permute-start.6
  72.1 1.5 collective-permute-start.7
  79.3 3.3 %all-to-all-start.4 = ((f32[8,3,2,128]{3,2,1,0:T(2,128)}), f32[8,3,2,128]{3,2,1,0:T(2,128)S(1)}, u32[]{:S(2)}, u32[]{:S(2)}) async-start(f32[8,3,2,128]{3,2,1,0:T(2,128)} %bitcast.67), calls=%async_computation.4 | async-start | bytes 49152 | tf_op jit(solution)/shard_map/all_to_all | solution.py:86
  82.7 5.5 %all-to-all-done.4 = f32[8,3,2,128]{3,2,1,0:T(2,128)S(1)} async-done(((f32[8,3,2,128]{3,2,1,0:T(2,128)}), f32[8,3,2,128]{3,2,1,0:T(2,128)S(1)}, u32[]{:S(2)}, u32[]{:S(2)}) %all-to-all-start.4) | async-done | bytes 24608 | tf_op jit(solution)/shard_map/all_to_all | solution.py:86
  88.2 1.5 collective-permute-start.8
  89.8 1.4 collective-permute-start.9
  96.0 3.3 %all-to-all-start.5 = ((f32[8,3,2,128]{3,2,1,0:T(2,128)}), f32[8,3,2,128]{3,2,1,0:T(2,128)S(1)}, u32[]{:S(2)}, u32[]{:S(2)}) async-start(f32[8,3,2,128]{3,2,1,0:T(2,128)} %bitcast.79), calls=%async_computation.5 | async-start | bytes 49152 | tf_op jit(solution)/shard_map/all_to_all | solution.py:86
  99.4 5.6 %all-to-all-done.5 = f32[8,3,2,128]{3,2,1,0:T(2,128)S(1)} async-done(((f32[8,3,2,128]{3,2,1,0:T(2,128)}), f32[8,3,2,128]{3,2,1,0:T(2,128)S(1)}, u32[]{:S(2)}, u32[]{:S(2)}) %all-to-all-start.5) | async-done | bytes 24608 | tf_op jit(solution)/shard_map/all_to_all | solution.py:86
  105.0 2.4 %collective-permute-start.10 = (f32[1,8,2,128]{3,2,1,0:T(2,128)S(1)}, f32[1,8,2,128]{3,2,1,0:T(2,128)S(1)}, u32[]{:S(2)}, u32[]{:S(2)}) collective-permute-start(f32[1,8,2,128]{3,2,1,0:T(2,128)S(1)} %get-tuple-element.89), channel_id=1, source_target_pairs={{0,8},{8,16},{16,24},{24,0},{1,9},{9,17},{17,25},{25,1},{2,10},{10... | collective-permute-start | bytes 24584 | tf_op jit(solution)/shard_map/ppermute | solution.py:16
  109.7 1.5 collective-permute-done.11
  114.6 3.3 %all-to-all-start.6 = ((f32[8,3,2,128]{3,2,1,0:T(2,128)}), f32[8,3,2,128]{3,2,1,0:T(2,128)S(1)}, u32[]{:S(2)}, u32[]{:S(2)}) async-start(f32[8,3,2,128]{3,2,1,0:T(2,128)} %bitcast.94), calls=%async_computation.6 | async-start | bytes 49152 | tf_op jit(solution)/shard_map/all_to_all | solution.py:86
  118.1 5.5 %all-to-all-done.6 = f32[8,3,2,128]{3,2,1,0:T(2,128)S(1)} async-done(((f32[8,3,2,128]{3,2,1,0:T(2,128)}), f32[8,3,2,128]{3,2,1,0:T(2,128)S(1)}, u32[]{:S(2)}, u32[]{:S(2)}) %all-to-all-start.6) | async-done | bytes 24608 | tf_op jit(solution)/shard_map/all_to_all | solution.py:86
  123.6 1.5 collective-permute-start.12
  125.2 1.4 collective-permute-start.13
  131.4 3.3 %all-to-all-start.7 = ((f32[8,3,2,128]{3,2,1,0:T(2,128)}), f32[8,3,2,128]{3,2,1,0:T(2,128)S(1)}, u32[]{:S(2)}, u32[]{:S(2)}) async-start(f32[8,3,2,128]{3,2,1,0:T(2,128)} %bitcast.106), calls=%async_computation.7 | async-start | bytes 49152 | tf_op jit(solution)/shard_map/all_to_all | solution.py:86
  134.8 5.6 %all-to-all-done.7 = f32[8,3,2,128]{3,2,1,0:T(2,128)S(1)} async-done(((f32[8,3,2,128]{3,2,1,0:T(2,128)}), f32[8,3,2,128]{3,2,1,0:T(2,128)S(1)}, u32[]{:S(2)}, u32[]{:S(2)}) %all-to-all-start.7) | async-done | bytes 24608 | tf_op jit(solution)/shard_map/all_to_all | solution.py:86
  141.8 1.5 collective-permute-start.15
  148.3 39.3 %psum.7 = f32[256]{0:T(256)S(1)} all-reduce(f32[256]{0:T(256)S(1)} %scatter_custom_fusion.12), channel_id=1, replica_groups=mesh['basin'=4,'blk'=8] {'basin','blk'}, use_global_device_ids=true, to_apply=%region_15.16 | all-reduce | flops 256 | bytes 2048 | tf_op jit(solution)/shard_map/psum | solution.py:121
  (207 shorter events, 49.7 us)
Async XLA Ops:
  0.6 2.3 %copy-start.1 = (f32[2,128,128]{2,1,0:T(8,128)S(1)}, f32[2,128,128]{2,1,0:T(8,128)}, u32[]{:S(2)}) copy-start(f32[2,128,128]{2,1,0:T(8,128)} %param.11) | copy-start | bytes 393220
  0.6 0.7 copy-start.6
  1.5 0.7 copy-start.5
  2.9 0.9 copy-start
  5.9 12.0 %all-to-all-start = ((f32[8,3,2,128]{3,2,1,0:T(2,128)}), f32[8,3,2,128]{3,2,1,0:T(2,128)S(1)}, u32[]{:S(2)}, u32[]{:S(2)}) async-start(f32[8,3,2,128]{3,2,1,0:T(2,128)} %bitcast.10), calls=%async_computation | async-start | bytes 49152 | tf_op jit(solution)/shard_map/all_to_all | solution.py:86
  12.3 0.7 copy-start.9
  17.9 4.6 %collective-permute-start = (f32[1,8,2,128]{3,2,1,0:T(2,128)S(1)}, f32[1,8,2,128]{3,2,1,0:T(2,128)S(1)}, u32[]{:S(2)}, u32[]{:S(2)}) collective-permute-start(f32[1,8,2,128]{3,2,1,0:T(2,128)S(1)} %get-tuple-element.104), channel_id=1, source_target_pairs={{0,8},{8,16},{16,24},{24,0},{1,9},{9,17},{17,25},{25,1},{2,10},{10... | collective-permute-start | bytes 24584 | tf_op jit(solution)/shard_map/ppermute | solution.py:16
  19.4 3.7 %collective-permute-start.1 = (f32[1,8,2,128]{3,2,1,0:T(2,128)S(1)}, f32[1,8,2,128]{3,2,1,0:T(2,128)S(1)}, u32[]{:S(2)}, u32[]{:S(2)}) collective-permute-start(f32[1,8,2,128]{3,2,1,0:T(2,128)S(1)} %get-tuple-element.105), channel_id=1, source_target_pairs={{8,0},{16,8},{24,16},{0,24},{9,1},{17,9},{25,17},{1,25},{10,2},{18... | collective-permute-start | bytes 24584 | tf_op jit(solution)/shard_map/ppermute | solution.py:19
  23.8 0.9 copy-start.2
  26.3 9.0 %all-to-all-start.1 = ((f32[8,3,2,128]{3,2,1,0:T(2,128)}), f32[8,3,2,128]{3,2,1,0:T(2,128)S(1)}, u32[]{:S(2)}, u32[]{:S(2)}) async-start(f32[8,3,2,128]{3,2,1,0:T(2,128)} %bitcast.25), calls=%async_computation.1 | async-start | bytes 49152 | tf_op jit(solution)/shard_map/all_to_all | solution.py:86
  35.3 4.6 %collective-permute-start.2 = (f32[1,8,2,128]{3,2,1,0:T(2,128)S(1)}, f32[1,8,2,128]{3,2,1,0:T(2,128)S(1)}, u32[]{:S(2)}, u32[]{:S(2)}) collective-permute-start(f32[1,8,2,128]{3,2,1,0:T(2,128)S(1)} %get-tuple-element.101), channel_id=1, source_target_pairs={{0,8},{8,16},{16,24},{24,0},{1,9},{9,17},{17,25},{25,1},{2,10},{10... | collective-permute-start | bytes 24584 | tf_op jit(solution)/shard_map/ppermute | solution.py:16
  37.7 3.7 %collective-permute-start.3 = (f32[1,8,2,128]{3,2,1,0:T(2,128)S(1)}, f32[1,8,2,128]{3,2,1,0:T(2,128)S(1)}, u32[]{:S(2)}, u32[]{:S(2)}) collective-permute-start(f32[1,8,2,128]{3,2,1,0:T(2,128)S(1)} %get-tuple-element.102), channel_id=1, source_target_pairs={{8,0},{16,8},{24,16},{0,24},{9,1},{17,9},{25,17},{1,25},{10,2},{18... | collective-permute-start | bytes 24584 | tf_op jit(solution)/shard_map/ppermute | solution.py:19
  44.9 9.0 %all-to-all-start.2 = ((f32[8,3,2,128]{3,2,1,0:T(2,128)}), f32[8,3,2,128]{3,2,1,0:T(2,128)S(1)}, u32[]{:S(2)}, u32[]{:S(2)}) async-start(f32[8,3,2,128]{3,2,1,0:T(2,128)} %bitcast.40), calls=%async_computation.2 | async-start | bytes 49152 | tf_op jit(solution)/shard_map/all_to_all | solution.py:86
  53.9 4.6 %collective-permute-start.4 = (f32[1,8,2,128]{3,2,1,0:T(2,128)S(1)}, f32[1,8,2,128]{3,2,1,0:T(2,128)S(1)}, u32[]{:S(2)}, u32[]{:S(2)}) collective-permute-start(f32[1,8,2,128]{3,2,1,0:T(2,128)S(1)} %get-tuple-element.98), channel_id=1, source_target_pairs={{0,8},{8,16},{16,24},{24,0},{1,9},{9,17},{17,25},{25,1},{2,10},{10... | collective-permute-start | bytes 24584 | tf_op jit(solution)/shard_map/ppermute | solution.py:16
  55.4 3.7 %collective-permute-start.5 = (f32[1,8,2,128]{3,2,1,0:T(2,128)S(1)}, f32[1,8,2,128]{3,2,1,0:T(2,128)S(1)}, u32[]{:S(2)}, u32[]{:S(2)}) collective-permute-start(f32[1,8,2,128]{3,2,1,0:T(2,128)S(1)} %get-tuple-element.99), channel_id=1, source_target_pairs={{8,0},{16,8},{24,16},{0,24},{9,1},{17,9},{25,17},{1,25},{10,2},{18... | collective-permute-start | bytes 24584 | tf_op jit(solution)/shard_map/ppermute | solution.py:19
  61.7 9.0 %all-to-all-start.3 = ((f32[8,3,2,128]{3,2,1,0:T(2,128)}), f32[8,3,2,128]{3,2,1,0:T(2,128)S(1)}, u32[]{:S(2)}, u32[]{:S(2)}) async-start(f32[8,3,2,128]{3,2,1,0:T(2,128)} %bitcast.52), calls=%async_computation.3 | async-start | bytes 49152 | tf_op jit(solution)/shard_map/all_to_all | solution.py:86
  70.7 4.6 %collective-permute-start.6 = (f32[1,8,2,128]{3,2,1,0:T(2,128)S(1)}, f32[1,8,2,128]{3,2,1,0:T(2,128)S(1)}, u32[]{:S(2)}, u32[]{:S(2)}) collective-permute-start(f32[1,8,2,128]{3,2,1,0:T(2,128)S(1)} %get-tuple-element.95), channel_id=1, source_target_pairs={{0,8},{8,16},{16,24},{24,0},{1,9},{9,17},{17,25},{25,1},{2,10},{10... | collective-permute-start | bytes 24584 | tf_op jit(solution)/shard_map/ppermute | solution.py:16
  72.1 3.7 %collective-permute-start.7 = (f32[1,8,2,128]{3,2,1,0:T(2,128)S(1)}, f32[1,8,2,128]{3,2,1,0:T(2,128)S(1)}, u32[]{:S(2)}, u32[]{:S(2)}) collective-permute-start(f32[1,8,2,128]{3,2,1,0:T(2,128)S(1)} %get-tuple-element.96), channel_id=1, source_target_pairs={{8,0},{16,8},{24,16},{0,24},{9,1},{17,9},{25,17},{1,25},{10,2},{18... | collective-permute-start | bytes 24584 | tf_op jit(solution)/shard_map/ppermute | solution.py:19
  79.3 9.0 %all-to-all-start.4 = ((f32[8,3,2,128]{3,2,1,0:T(2,128)}), f32[8,3,2,128]{3,2,1,0:T(2,128)S(1)}, u32[]{:S(2)}, u32[]{:S(2)}) async-start(f32[8,3,2,128]{3,2,1,0:T(2,128)} %bitcast.67), calls=%async_computation.4 | async-start | bytes 49152 | tf_op jit(solution)/shard_map/all_to_all | solution.py:86
  88.2 4.6 %collective-permute-start.8 = (f32[1,8,2,128]{3,2,1,0:T(2,128)S(1)}, f32[1,8,2,128]{3,2,1,0:T(2,128)S(1)}, u32[]{:S(2)}, u32[]{:S(2)}) collective-permute-start(f32[1,8,2,128]{3,2,1,0:T(2,128)S(1)} %get-tuple-element.92), channel_id=1, source_target_pairs={{0,8},{8,16},{16,24},{24,0},{1,9},{9,17},{17,25},{25,1},{2,10},{10... | collective-permute-start | bytes 24584 | tf_op jit(solution)/shard_map/ppermute | solution.py:16
  89.8 3.7 %collective-permute-start.9 = (f32[1,8,2,128]{3,2,1,0:T(2,128)S(1)}, f32[1,8,2,128]{3,2,1,0:T(2,128)S(1)}, u32[]{:S(2)}, u32[]{:S(2)}) collective-permute-start(f32[1,8,2,128]{3,2,1,0:T(2,128)S(1)} %get-tuple-element.93), channel_id=1, source_target_pairs={{8,0},{16,8},{24,16},{0,24},{9,1},{17,9},{25,17},{1,25},{10,2},{18... | collective-permute-start | bytes 24584 | tf_op jit(solution)/shard_map/ppermute | solution.py:19
  96.0 9.0 %all-to-all-start.5 = ((f32[8,3,2,128]{3,2,1,0:T(2,128)}), f32[8,3,2,128]{3,2,1,0:T(2,128)S(1)}, u32[]{:S(2)}, u32[]{:S(2)}) async-start(f32[8,3,2,128]{3,2,1,0:T(2,128)} %bitcast.79), calls=%async_computation.5 | async-start | bytes 49152 | tf_op jit(solution)/shard_map/all_to_all | solution.py:86
  105.0 4.6 %collective-permute-start.10 = (f32[1,8,2,128]{3,2,1,0:T(2,128)S(1)}, f32[1,8,2,128]{3,2,1,0:T(2,128)S(1)}, u32[]{:S(2)}, u32[]{:S(2)}) collective-permute-start(f32[1,8,2,128]{3,2,1,0:T(2,128)S(1)} %get-tuple-element.89), channel_id=1, source_target_pairs={{0,8},{8,16},{16,24},{24,0},{1,9},{9,17},{17,25},{25,1},{2,10},{10... | collective-permute-start | bytes 24584 | tf_op jit(solution)/shard_map/ppermute | solution.py:16
  107.5 3.7 %collective-permute-start.11 = (f32[1,8,2,128]{3,2,1,0:T(2,128)S(1)}, f32[1,8,2,128]{3,2,1,0:T(2,128)S(1)}, u32[]{:S(2)}, u32[]{:S(2)}) collective-permute-start(f32[1,8,2,128]{3,2,1,0:T(2,128)S(1)} %get-tuple-element.90), channel_id=1, source_target_pairs={{8,0},{16,8},{24,16},{0,24},{9,1},{17,9},{25,17},{1,25},{10,2},{18... | collective-permute-start | bytes 24584 | tf_op jit(solution)/shard_map/ppermute | solution.py:19
  114.6 9.0 %all-to-all-start.6 = ((f32[8,3,2,128]{3,2,1,0:T(2,128)}), f32[8,3,2,128]{3,2,1,0:T(2,128)S(1)}, u32[]{:S(2)}, u32[]{:S(2)}) async-start(f32[8,3,2,128]{3,2,1,0:T(2,128)} %bitcast.94), calls=%async_computation.6 | async-start | bytes 49152 | tf_op jit(solution)/shard_map/all_to_all | solution.py:86
  123.6 4.6 %collective-permute-start.12 = (f32[1,8,2,128]{3,2,1,0:T(2,128)S(1)}, f32[1,8,2,128]{3,2,1,0:T(2,128)S(1)}, u32[]{:S(2)}, u32[]{:S(2)}) collective-permute-start(f32[1,8,2,128]{3,2,1,0:T(2,128)S(1)} %get-tuple-element.86), channel_id=1, source_target_pairs={{0,8},{8,16},{16,24},{24,0},{1,9},{9,17},{17,25},{25,1},{2,10},{10... | collective-permute-start | bytes 24584 | tf_op jit(solution)/shard_map/ppermute | solution.py:16
  125.2 3.7 %collective-permute-start.13 = (f32[1,8,2,128]{3,2,1,0:T(2,128)S(1)}, f32[1,8,2,128]{3,2,1,0:T(2,128)S(1)}, u32[]{:S(2)}, u32[]{:S(2)}) collective-permute-start(f32[1,8,2,128]{3,2,1,0:T(2,128)S(1)} %get-tuple-element.87), channel_id=1, source_target_pairs={{8,0},{16,8},{24,16},{0,24},{9,1},{17,9},{25,17},{1,25},{10,2},{18... | collective-permute-start | bytes 24584 | tf_op jit(solution)/shard_map/ppermute | solution.py:19
  131.4 9.0 %all-to-all-start.7 = ((f32[8,3,2,128]{3,2,1,0:T(2,128)}), f32[8,3,2,128]{3,2,1,0:T(2,128)S(1)}, u32[]{:S(2)}, u32[]{:S(2)}) async-start(f32[8,3,2,128]{3,2,1,0:T(2,128)} %bitcast.106), calls=%async_computation.7 | async-start | bytes 49152 | tf_op jit(solution)/shard_map/all_to_all | solution.py:86
  140.4 4.6 %collective-permute-start.14 = (f32[1,8,2,128]{3,2,1,0:T(2,128)S(1)}, f32[1,8,2,128]{3,2,1,0:T(2,128)S(1)}, u32[]{:S(2)}, u32[]{:S(2)}) collective-permute-start(f32[1,8,2,128]{3,2,1,0:T(2,128)S(1)} %get-tuple-element.83), channel_id=1, source_target_pairs={{0,8},{8,16},{16,24},{24,0},{1,9},{9,17},{17,25},{25,1},{2,10},{10... | collective-permute-start | bytes 24584 | tf_op jit(solution)/shard_map/ppermute | solution.py:16
  141.8 3.7 %collective-permute-start.15 = (f32[1,8,2,128]{3,2,1,0:T(2,128)S(1)}, f32[1,8,2,128]{3,2,1,0:T(2,128)S(1)}, u32[]{:S(2)}, u32[]{:S(2)}) collective-permute-start(f32[1,8,2,128]{3,2,1,0:T(2,128)S(1)} %get-tuple-element.84), channel_id=1, source_target_pairs={{8,0},{16,8},{24,16},{0,24},{9,1},{17,9},{25,17},{1,25},{10,2},{18... | collective-permute-start | bytes 24584 | tf_op jit(solution)/shard_map/ppermute | solution.py:19
  146.4 1.0 copy-start.3
  146.6 1.0 copy-start.4
  (3 other events, 2.0 us)
where the time goes:
time: 190 us; the launch traced here: 189 us
  waiting for transfers between devices  57.5 us (30%)
  starting transfers between devices  53.5 us (28%)
  blocking collectives  39.3 us (21%)
  local copies, waits for them, and re-layouts  29.3 us (15%)
  other arithmetic  7.09 us (4%)
  between operations  2.13 us (1%)
    all_to_all x8, waiting for transfers between devices, collect(): lax.all_to_all(outgoing, 'blk', split_axis=0, concat_axis=0, tiled=True)  43.8 us
    psum x1, blocking collectives, shards(): whole = lax.psum(spread, ('basin', 'blk'))  39.3 us
    all_to_all x8, starting transfers between devices, collect(): lax.all_to_all(outgoing, 'blk', split_axis=0, concat_axis=0, tiled=True)  29.7 us
    ppermute x8, starting transfers between devices, with_halo(): lax.ppermute(lax.slice_in_dim(block, block.shape[dim] - width, None, axis...  13.9 us
    ppermute x8, starting transfers between devices, with_halo(): lax.ppermute(lax.slice_in_dim(block, 0, width, axis=dim), axis, backward)  9.9 us
    ppermute x8, waiting for transfers between devices, with_halo(): lax.ppermute(lax.slice_in_dim(block, block.shape[dim] - width, None, axis...  7.57 us
    ppermute x8, waiting for transfers between devices, with_halo(): lax.ppermute(lax.slice_in_dim(block, 0, width, axis=dim), axis, backward)  6.13 us
    unnamed x30, local copies, waits for them, and re-layouts  5.41 us
  transfers between devices with their start and end apart: 24, of which 24 were waited for; matrix products, arithmetic and copies ran while one was open for 3% of the time, Pallas kernels for 0%

commit v1 on v0

v1 whole, which is shorter than its diff:
```python
import functools

import jax
import jax.numpy as jnp
from jax import lax
from jax.experimental import pallas as pl
from jax.experimental.pallas import tpu as pltpu
from jax.sharding import PartitionSpec as P

coupling = 0.5
prior_weight = 0.5
MESH = pl.DeviceIdType.MESH
PAD = 8
PAIR = 2


def kernel(
    basins,
    groups,
    owned,
    near_ref,
    subfault_ref,
    gauge_ref,
    misfit_ref,
    terminal_ref,
    depth_ref,
    wet_ref,
    basis_ref,
    surface_ref,
    mine_ref,
    terminal,
    depth,
    wet,
    basis,
    wet_f,
    across,
    along,
    across_md,
    along_md,
    across_flow,
    along_flow,
    edges,
    sums_out,
    sums_in,
    chosen,
    load_sem,
    send_sem,
    recv_sem,
    sums_sem,
    *halo_buffers,
):
    slots, side, _ = terminal.shape
    steps = misfit_ref.shape[0]
    outs, landings = halo_buffers[:steps], halo_buffers[steps:]
    patterns = basis.shape[1]
    entries = slots * 4
    devices = basins * groups
    peers = 3 * groups
    basin = lax.axis_index("basin")
    group = lax.axis_index("blk")
    me = basin * groups + group
    own_place = groups + group

    loads = [
        pltpu.make_async_copy(terminal_ref, terminal, load_sem.at[0]),
        pltpu.make_async_copy(wet_ref, wet, load_sem.at[1]),
        pltpu.make_async_copy(depth_ref, depth, load_sem.at[2]),
        pltpu.make_async_copy(basis_ref, basis, load_sem.at[3]),
    ]
    for load in loads:
        load.start()

    barrier = pltpu.get_barrier_semaphore()

    @pl.loop(1, devices)
    def _(k):
        other = (me + k) % devices
        pl.semaphore_signal(
            barrier, inc=1, device_id=(other // groups, other % groups), device_id_type=MESH
        )

    spare = peers * PAIR
    named = [near_ref[e // 4, e % 4] for e in range(entries)]
    there = [n >= 0 for n in named]
    safe = [jnp.maximum(n, 0) for n in named]
    holder = [n // slots for n in safe]
    source = [safe[e] % slots * 4 + (e % 4) + 1 - 2 * (e % 2) for e in range(entries)]
    local = [h == me for h in holder]
    heading = [(h // groups - basin + 1 + basins) % basins for h in holder]
    place = [
        jnp.where(there[e], heading[e] * groups + holder[e] % groups, -1) for e in range(entries)
    ]
    lookup = []
    for e in range(entries):
        rank = 0
        for f in range(entries):
            if f != e:
                earlier = (place[f] == place[e]) & (source[f] < source[e])
                rank = jnp.where(earlier, 1, rank)
        index = jnp.where(local[e], spare + source[e], place[e] * PAIR + rank)
        lookup.append(jnp.where(there[e], index, spare + entries))

    @pl.loop(0, peers)
    def _(p):
        low = entries
        high = entries
        for e in range(entries):
            high = jnp.where(place[e] == p, e, high)
        for e in reversed(range(entries)):
            low = jnp.where(place[e] == p, e, low)
        chosen[p * PAIR] = low
        chosen[p * PAIR + 1] = high

    gauge = gauge_ref[...].reshape(1, -1)
    count = gauge.shape[1]
    row_hot = jnp.where(
        lax.broadcasted_iota(jnp.int32, (slots * side, count), 0) == gauge // side, 1.0, 0.0
    )
    column_hot = lax.broadcasted_iota(jnp.int32, (side, count), 0) == gauge % side

    def injected(t):
        weights = jnp.where(column_hot, misfit_ref[t : t + 1, :], 0.0)
        return lax.dot_general(
            row_hot,
            weights,
            (((1,), (1,)), ((), ())),
            precision=lax.Precision.HIGHEST,
            preferred_element_type=jnp.float32,
        ).reshape(slots, side, side)

    for ref in (across_flow, along_flow):
        ref[...] = jnp.zeros_like(ref)
    edges[...] = jnp.zeros_like(edges)

    inside = slice(PAD, PAD + side)
    for load in loads[:3]:
        load.wait()
    for s in range(slots):
        m = wet[s].astype(jnp.float32)
        wet_f[s] = m
        md = m * depth[s] * (coupling * 0.5)
        along_md[s, inside] = md
        across_md[s, inside] = md.T

    def sends(t, out, landing):
        @pl.loop(1, peers)
        def _(k):
            p = (own_place + k) % peers
            p_heading = p // groups
            p_group = p % groups
            p_basin = (basin + p_heading - 1 + basins) % basins
            landing_at = (2 - p_heading) * groups + group
            pltpu.make_async_remote_copy(
                src_ref=out.at[pl.ds(p * PAIR, PAIR)],
                dst_ref=landing.at[pl.ds(landing_at * PAIR, PAIR)],
                send_sem=send_sem.at[t],
                recv_sem=recv_sem.at[t],
                device_id=(p_basin, p_group),
                device_id_type=MESH,
            ).start()

    def await_bytes(ref, sem):
        pltpu.make_async_copy(ref, ref, sem).wait()

    rest = slice(PAD - 1, PAD + side + 1)
    before = slice(PAD - 2, PAD + side)
    after = slice(PAD, PAD + side + 2)
    for t in range(steps):
        out, landing = outs[t], landings[t]
        force = injected(t)
        for s in range(slots):
            surface = terminal[s] if t == 0 else surface_ref[s]
            masked = wet_f[s] * (surface + force[s])
            along[s, inside] = masked
            across[s, inside] = masked.T
            for at, field, depths in ((0, across, across_md), (2, along, along_md)):
                edges[s * 4 + at, 0:2] = field[s, PAD : PAD + 2]
                edges[s * 4 + at + 1, 0:2] = field[s, PAD + side - 2 : PAD + side]
                if t == 0:
                    edges[s * 4 + at, 2:3] = depths[s, PAD : PAD + 1]
                    edges[s * 4 + at + 1, 2:3] = depths[s, PAD + side - 1 : PAD + side]
        width = 4 if t == 0 else 2
        for e in range(entries + 1):
            landing[spare + e] = edges[e, 0:width]
        for i in range(peers * PAIR):
            out[i] = edges[chosen[i], 0:width]
        if t == 0:
            pl.semaphore_wait(barrier, devices - 1)
        sends(t, out, landing)
        await_bytes(landing.at[pl.ds(0, (peers - 1) * PAIR)], recv_sem.at[t])
        for e in range(entries):
            s, at = e // 4, e % 4
            field, depths = (across, across_md) if at < 2 else (along, along_md)
            got = landing[lookup[e]]
            if at % 2 == 0:
                field[s, PAD - 2 : PAD] = got[0:2]
                if t == 0:
                    depths[s, PAD - 1 : PAD] = got[2:3]
            else:
                field[s, PAD + side : PAD + side + 2] = got[0:2]
                if t == 0:
                    depths[s, PAD + side : PAD + side + 1] = got[2:3]
        for s in range(slots):
            for field, depths, flow in (
                (across, across_md, across_flow),
                (along, along_md, along_flow),
            ):
                flow[s, rest] += depths[s, rest] * (field[s, after] - field[s, before])

            def gradient(flow):
                return (coupling * 0.5) * (
                    flow[s, PAD + 1 : PAD + side + 1] - flow[s, PAD - 1 : PAD + side - 1]
                )

            surface_ref[s] = along[s, inside] + (gradient(across_flow).T + gradient(along_flow))

    loads[3].wait()
    partial = []
    for s in range(slots):
        for j in range(patterns):
            down = jnp.sum(basis[s, j] * surface_ref[s], axis=0, keepdims=True)
            partial.append(jnp.sum(down, axis=1, keepdims=True))
    lanes = sums_out.shape[2]
    lane = lax.broadcasted_iota(jnp.int32, (1, lanes), 1)

    def share(device):
        row = jnp.zeros((1, lanes), jnp.float32)
        for e in range(slots * patterns):
            spot = subfault_ref[e // patterns, e % patterns] - device * owned
            row = row + jnp.where((lane == spot) & (lane < owned), partial[e], 0.0)
        return row

    @pl.loop(1, devices)
    def _(k):
        other = (me + k) % devices
        sums_out[other] = share(other)
        pltpu.make_async_remote_copy(
            src_ref=sums_out.at[other],
            dst_ref=sums_in.at[me],
            send_sem=sums_sem.at[0],
            recv_sem=sums_sem.at[1],
            device_id=(other // groups, other % groups),
            device_id_type=MESH,
        ).start()

    sums_in[me] = share(me)
    await_bytes(sums_in.at[pl.ds(0, devices - 1)], sums_sem.at[1])
    mine_ref[...] = jnp.sum(sums_in[...], axis=0)
    await_bytes(sums_out.at[pl.ds(0, devices - 1)], sums_sem.at[0])
    for t in range(steps):
        await_bytes(outs[t].at[pl.ds(0, (peers - 1) * PAIR)], send_sem.at[t])


def shards(
    terminal,
    depth,
    wet_cells,
    neighbours,
    gauge_cell,
    misfit,
    basis,
    subfault_index,
    source,
    background,
    step_size,
):
    slots, side, _ = terminal.shape
    steps = misfit.shape[0]
    owned = source.shape[0]
    basins = lax.axis_size("basin")
    groups = lax.axis_size("blk")
    devices = basins * groups
    rows = 3 * groups * PAIR
    entries = slots * 4
    kept = rows + entries + 1
    lanes = -(-owned // 128) * 128
    widths = [4] + [2] * (steps - 1)
    f32 = jnp.float32
    padded = pltpu.VMEM((slots, side + 2 * PAD, side), f32)
    smem = pl.BlockSpec(memory_space=pltpu.SMEM)
    vmem = pl.BlockSpec(memory_space=pltpu.VMEM)
    hbm = pl.BlockSpec(memory_space=pl.ANY)
    surface, mine = pl.pallas_call(
        functools.partial(kernel, basins, groups, owned),
        out_shape=(
            jax.ShapeDtypeStruct(terminal.shape, f32),
            jax.ShapeDtypeStruct((1, lanes), f32),
        ),
        in_specs=[smem, smem, vmem, vmem, hbm, hbm, hbm, hbm],
        out_specs=(vmem, vmem),
        scratch_shapes=[
            pltpu.VMEM(terminal.shape, f32),
            pltpu.VMEM(terminal.shape, f32),
            pltpu.VMEM(terminal.shape, jnp.int32),
            pltpu.VMEM(basis.shape, f32),
            pltpu.VMEM(terminal.shape, f32),
            padded,
            padded,
            padded,
            padded,
            padded,
            padded,
            pltpu.VMEM((entries + 1, 4, side), f32),
            pltpu.VMEM((devices, 1, lanes), f32),
            pltpu.VMEM((devices, 1, lanes), f32),
            pltpu.SMEM((rows,), jnp.int32),
            pltpu.SemaphoreType.DMA((4,)),
            pltpu.SemaphoreType.DMA((steps,)),
            pltpu.SemaphoreType.DMA((steps,)),
            pltpu.SemaphoreType.DMA((2,)),
            *[pltpu.VMEM((rows, width, side), f32) for width in widths],
            *[pltpu.VMEM((kept, width, side), f32) for width in widths],
        ],
        compiler_params=pltpu.CompilerParams(
            collective_id=0, has_side_effects=True, vmem_limit_bytes=32 * 1024 * 1024
        ),
        cost_estimate=pl.CostEstimate(flops=4_000_000, bytes_accessed=1_100_000, transcendentals=0),
        name="adjoint",
    )(neighbours, subfault_index, gauge_cell, misfit, terminal, depth, wet_cells, basis)
    gradient = prior_weight * (source - background) + mine[0, :owned]
    return (surface, source - step_size[0] * gradient)


def solution(mesh):
    in_specs = (
        P(("basin", "blk"), None, None),
        P(("basin", "blk"), None, None),
        P(("basin", "blk"), None, None),
        P(("basin", "blk"), None),
        P(("basin", "blk")),
        P(None, ("basin", "blk")),
        P(("basin", "blk"), None, None, None),
        P(("basin", "blk"), None),
        P(("basin", "blk")),
        P(("basin", "blk")),
        P(),
    )
    out_specs = (P(("basin", "blk"), None, None), P(("basin", "blk")))
    return jax.shard_map(shards, mesh=mesh, in_specs=in_specs, out_specs=out_specs, check_vma=False)
```

time: 190 us -> 42.6 us (0.22)
  waiting for transfers between devices: 57.5 us -> 0 us
  starting transfers between devices: 53.5 us -> 0 us
  blocking collectives: 39.3 us -> 0 us
  Pallas kernels: 0 us -> 32.8 us
  local copies, waits for them, and re-layouts: 29.3 us -> 7.75 us
  other arithmetic: 7.09 us -> 0.52 us
    all_to_all x8 -> x0, waiting for transfers between devices: 43.8 us -> none  [collect(): lax.all_to_all(outgoing, 'blk', split_axis=0, concat_axis=0, tiled=True)]
    psum x1 -> x0, blocking collectives: 39.3 us -> none  [shards(): whole = lax.psum(spread, ('basin', 'blk'))]
    pallas_call x0 -> x1, Pallas kernels: none -> 32.8 us  [shards(): pl.pallas_call(functools.partial(kernel, basins, groups, owned), out_shap...]
    all_to_all x8 -> x0, starting transfers between devices: 29.7 us -> none  [collect(): lax.all_to_all(outgoing, 'blk', split_axis=0, concat_axis=0, tiled=True)]
    ppermute x16 -> x0, starting transfers between devices: 23.8 us -> none  [the longest x8 13.9 us: with_halo(): lax.ppermute(lax.slice_in_dim(block, block.shape[dim] - width, None, axis...]
    ppermute x16 -> x0, waiting for transfers between devices: 13.7 us -> none  [the longest x8 7.57 us: with_halo(): lax.ppermute(lax.slice_in_dim(block, block.shape[dim] - width, None, axis...]
    gather x16 -> x0, local copies, waits for them, and re-layouts: 8.91 us -> none  [the longest x8 4.46 us: collect(): packed[source_edge]]
    slice x48 -> x0, local copies, waits for them, and re-layouts: 7.02 us -> none  [the longest x8 4.88 us: collect(): outgoing = outgoing[:-1].reshape(group_count, 3, slot_count, block_side)]
  transfers between devices with their start and end apart: 24 -> 0, of which waited for: 24 -> 0; matrix products, arithmetic and copies ran while one was open for 3% -> 0% of each run, Pallas kernels for 0% -> 0%
where the time goes in v1:
time: 42.6 us; the launch traced here: 42.3 us
  Pallas kernels  32.8 us (77%)
  local copies, waits for them, and re-layouts  7.75 us (18%)
  between operations  1.32 us (3%)
  other arithmetic  0.52 us (1%)
    pallas_call x1, Pallas kernels, shards(): pl.pallas_call(functools.partial(kernel, basins, groups, owned), out_shap...  32.8 us
    unnamed x21, local copies, waits for them, and re-layouts  7.75 us

profile of v1, /device:TPU:0, one launch (start us, length us, event | category | flops | bytes accessed | tf_op | source)
XLA Modules:
  0.0 42.3 jit_solution(1214324734562608360)
XLA Ops:
  0.6 0.0 copy-start
  0.6 1.0 %copy-done = f32[2,4,128,128]{3,2,1,0:T(8,128)S(1)} copy-done((f32[2,4,128,128]{3,2,1,0:T(8,128)S(1)}, f32[2,4,128,128]{3,2,1,0:T(8,128)}, u32[]{:S(2)}) %copy-start) | copy-done | bytes 524312
  1.7 0.0 copy-start.1
  1.7 0.9 %copy-done.1 = f32[2,128,128]{2,1,0:T(8,128)S(1)} copy-done((f32[2,128,128]{2,1,0:T(8,128)S(1)}, f32[2,128,128]{2,1,0:T(8,128)}, u32[]{:S(2)}) %copy-start.1) | copy-done | bytes 131096
  2.6 0.0 copy-start.2
  2.6 0.9 %copy-done.2 = f32[2,128,128]{2,1,0:T(8,128)S(1)} copy-done((f32[2,128,128]{2,1,0:T(8,128)S(1)}, f32[2,128,128]{2,1,0:T(8,128)}, u32[]{:S(2)}) %copy-start.2) | copy-done | bytes 131096
  3.5 0.0 copy-start.3
  3.5 0.9 %copy-done.3 = s32[2,128,128]{2,1,0:T(8,128)S(1)} copy-done((s32[2,128,128]{2,1,0:T(8,128)S(1)}, s32[2,128,128]{2,1,0:T(8,128)}, u32[]{:S(2)}) %copy-start.3) | copy-done | bytes 131096
  4.4 0.0 copy-start.4
  4.4 0.7 %copy-done.4 = f32[4,32]{1,0:T(4,128)S(1)} copy-done((f32[4,32]{1,0:T(4,128)S(1)}, f32[4,32]{1,0:T(4,128)}, u32[]{:S(2)}) %copy-start.4) | copy-done | bytes 536
  5.1 0.0 copy-start.5
  5.1 0.7 %copy-done.5 = s32[2,4]{1,0:T(2,128)S(1)} copy-done((s32[2,4]{1,0:T(2,128)S(1)}, s32[2,4]{1,0:T(2,128)}, u32[]{:S(2)}) %copy-start.5) | copy-done | bytes 56
  5.8 0.0 copy-start.6
  5.8 0.7 %copy-done.6 = s32[2,4]{1,0:T(2,128)S(1)} copy-done((s32[2,4]{1,0:T(2,128)S(1)}, s32[2,4]{1,0:T(2,128)}, u32[]{:S(2)}) %copy-start.6) | copy-done | bytes 56
  6.4 0.0 copy-start.7
  6.4 0.7 %copy-done.7 = s32[32]{0:T(128)S(1)} copy-done((s32[32]{0:T(128)S(1)}, s32[32]{0:T(128)}, u32[]{:S(2)}) %copy-start.7) | copy-done | bytes 152
  7.1 32.8 %adjoint.1 = (f32[2,128,128]{2,1,0:T(8,128)S(1)}, f32[1,128]{1,0:T(1,128)S(1)}) custom-call(s32[2,4]{1,0:T(2,128)S(1)} %copy-done.5, s32[2,4]{1,0:T(2,128)S(1)} %copy-done.6, s32[32]{0:T(128)S(1)} %copy-done.7, f32[4,32]{1,0:T(4,128)S(1)} %copy-done.4, f32[2,128,128]{2,1,0:T(8,128)S(1)} %copy-done.1, f32[2,128,128]{2,1,0:T(8,128)S(1)} %copy-done.2, ...), custom_call_target="tpu_custom_call" | custom-call | flops 4000000 | bytes 1100000 | tf_op jit(solution)/shard_map/adjoint/pallas_call | solution.py:283
  40.5 0.0 copy-start.8
  40.5 0.0 copy-start.9
  40.5 0.6 %copy-done.8 = f32[8]{0:T(128)S(1)} copy-done((f32[8]{0:T(128)S(1)}, f32[8]{0:T(128)}, u32[]{:S(2)}) %copy-start.8) | copy-done | bytes 56
  41.1 0.0 copy-done.9
  41.2 0.5 %fusion.1 = f32[8]{0:T(128)} fusion(f32[8]{0:T(128)S(1)} %copy-done.8, f32[1,128]{1,0:T(1,128)S(1)} %get-tuple-element.5, f32[8]{0:T(128)S(1)} %copy-done.9, f32[]{:T(128)} %bitcast.7), kind=kLoop, calls=%fused_computation.2 | loop fusion | flops 40 | bytes 132 | tf_op jit(solution)/shard_map/sub | solution.py:321
  41.7 0.7 %copy.15 = f32[2,128,128]{2,1,0:T(8,128)} copy(f32[2,128,128]{2,1,0:T(8,128)S(1)} %get-tuple-element.8) | data formatting | bytes 262144
Async XLA Ops:
  0.6 1.0 %copy-start = (f32[2,4,128,128]{3,2,1,0:T(8,128)S(1)}, f32[2,4,128,128]{3,2,1,0:T(8,128)}, u32[]{:S(2)}) copy-start(f32[2,4,128,128]{3,2,1,0:T(8,128)} %basis_ref.1) | copy-start | bytes 1572868
  1.7 0.9 %copy-start.1 = (f32[2,128,128]{2,1,0:T(8,128)S(1)}, f32[2,128,128]{2,1,0:T(8,128)}, u32[]{:S(2)}) copy-start(f32[2,128,128]{2,1,0:T(8,128)} %terminal_ref.1) | copy-start | bytes 393220
  2.6 0.9 %copy-start.2 = (f32[2,128,128]{2,1,0:T(8,128)S(1)}, f32[2,128,128]{2,1,0:T(8,128)}, u32[]{:S(2)}) copy-start(f32[2,128,128]{2,1,0:T(8,128)} %depth_ref.1) | copy-start | bytes 393220
  3.5 0.9 %copy-start.3 = (s32[2,128,128]{2,1,0:T(8,128)S(1)}, s32[2,128,128]{2,1,0:T(8,128)}, u32[]{:S(2)}) copy-start(s32[2,128,128]{2,1,0:T(8,128)} %wet_ref.1) | copy-start | bytes 393220
  4.4 0.7 %copy-start.4 = (f32[4,32]{1,0:T(4,128)S(1)}, f32[4,32]{1,0:T(4,128)}, u32[]{:S(2)}) copy-start(f32[4,32]{1,0:T(4,128)} %misfit_ref.1) | copy-start | bytes 1540
  5.1 0.7 %copy-start.5 = (s32[2,4]{1,0:T(2,128)S(1)}, s32[2,4]{1,0:T(2,128)}, u32[]{:S(2)}) copy-start(s32[2,4]{1,0:T(2,128)} %near_ref.1) | copy-start | bytes 100
  5.8 0.7 %copy-start.6 = (s32[2,4]{1,0:T(2,128)S(1)}, s32[2,4]{1,0:T(2,128)}, u32[]{:S(2)}) copy-start(s32[2,4]{1,0:T(2,128)} %subfault_ref.1) | copy-start | bytes 100
  6.4 0.7 %copy-start.7 = (s32[32]{0:T(128)S(1)}, s32[32]{0:T(128)}, u32[]{:S(2)}) copy-start(s32[32]{0:T(128)} %gauge_ref.1) | copy-start | bytes 388
  40.5 0.7 %copy-start.8 = (f32[8]{0:T(128)S(1)}, f32[8]{0:T(128)}, u32[]{:S(2)}) copy-start(f32[8]{0:T(128)} %param.19) | copy-start | bytes 100
  40.5 0.7 %copy-start.9 = (f32[8]{0:T(128)S(1)}, f32[8]{0:T(128)}, u32[]{:S(2)}) copy-start(f32[8]{0:T(128)} %param.20) | copy-start | bytes 100

commit v2 on v1

v2 whole, which is shorter than its diff:
```python
import functools

import jax
import jax.numpy as jnp
from jax import lax
from jax.experimental import pallas as pl
from jax.experimental.pallas import tpu as pltpu
from jax.sharding import PartitionSpec as P

coupling = 0.5
prior_weight = 0.5
MESH = pl.DeviceIdType.MESH
PAD = 8
PAIR = 2


def wrapped(value, count):
    return jnp.where(value >= count, value - count, value)


def split_exact(x):
    high = x.astype(jnp.bfloat16)
    left = x - high.astype(jnp.float32)
    middle = left.astype(jnp.bfloat16)
    return high, middle, (left - middle.astype(jnp.float32)).astype(jnp.bfloat16)


def kernel(
    basins,
    groups,
    near_hbm,
    subfault_hbm,
    step_hbm,
    gauge_hbm,
    misfit_hbm,
    source_hbm,
    background_hbm,
    terminal_hbm,
    wet_hbm,
    depth_hbm,
    basis_hbm,
    surface_ref,
    updated_ref,
    near_ref,
    subfault_ref,
    step_ref,
    gauge_ref,
    misfit_ref,
    source_ref,
    background_ref,
    terminal,
    wet,
    depth,
    basis,
    wet_f,
    forces,
    across,
    along,
    across_md,
    along_md,
    across_flow,
    along_flow,
    edges,
    sums_out,
    sums_in,
    chosen,
    load_sem,
    send_sem,
    recv_sem,
    sums_sem,
    *halo_buffers,
):
    slots, side, _ = terminal.shape
    steps = misfit_ref.shape[0]
    outs, landings = halo_buffers[:steps], halo_buffers[steps:]
    patterns = basis.shape[1]
    owned = source_ref.shape[0]
    entries = slots * 4
    devices = basins * groups
    peers = 3 * groups
    basin = lax.axis_index("basin")
    group = lax.axis_index("blk")
    me = basin * groups + group

    pairs = (
        (near_hbm, near_ref),
        (subfault_hbm, subfault_ref),
        (step_hbm, step_ref),
        (gauge_hbm, gauge_ref),
        (misfit_hbm, misfit_ref),
        (source_hbm, source_ref),
        (background_hbm, background_ref),
        (terminal_hbm, terminal),
        (wet_hbm, wet),
        (depth_hbm, depth),
        (basis_hbm, basis),
    )
    loads = [pltpu.make_async_copy(a, b, load_sem.at[i]) for i, (a, b) in enumerate(pairs)]
    for load in loads:
        load.start()

    def each_peer(shifts, body):
        for shift in shifts:
            there = wrapped(basin + shift, basins)

            @pl.loop(1 if shift == 0 else 0, groups, unroll=min(groups, 8))
            def _(k):
                body(shift, there, wrapped(group + k, groups))

    barrier = pltpu.get_barrier_semaphore()

    def greet(shift, there, other):
        pl.semaphore_signal(barrier, inc=1, device_id=(there, other), device_id_type=MESH)

    each_peer(range(basins), greet)

    for ref in (across_flow, along_flow, edges):
        ref[...] = jnp.zeros_like(ref)

    loads[3].wait()
    loads[4].wait()
    gauge = gauge_ref[...].reshape(1, -1)
    count = gauge.shape[1]
    row_hot = lax.broadcasted_iota(jnp.int32, (slots * side, count), 0) == gauge // side
    row_hot = jnp.where(row_hot, 1.0, 0.0).astype(jnp.bfloat16)
    column_hot = lax.broadcasted_iota(jnp.int32, (side, count), 0) == gauge % side

    def injected(t):
        weights = jnp.where(column_hot, misfit_ref[t : t + 1, :], 0.0)
        total = None
        for part in split_exact(weights):
            term = lax.dot_general(
                row_hot, part, (((1,), (1,)), ((), ())), preferred_element_type=jnp.float32
            )
            total = term if total is None else total + term
        forces[...] = total.reshape(slots, side, side)

    injected(0)

    loads[0].wait()
    spare = peers * PAIR
    named = [near_ref[e // 4, e % 4] for e in range(entries)]
    present = [n >= 0 for n in named]
    safe = [jnp.maximum(n, 0) for n in named]
    holder = [n // slots for n in safe]
    origin = [safe[e] % slots * 4 + (e % 4) + 1 - 2 * (e % 2) for e in range(entries)]
    local = [h == me for h in holder]
    heading = [(h // groups - basin + 1 + basins) % basins for h in holder]
    place = [
        jnp.where(present[e], heading[e] * groups + holder[e] % groups, -1)
        for e in range(entries)
    ]
    lookup = []
    for e in range(entries):
        rank = 0
        for f in range(entries):
            if f != e:
                earlier = (place[f] == place[e]) & (origin[f] < origin[e])
                rank = jnp.where(earlier, 1, rank)
        index = jnp.where(local[e], spare + origin[e], place[e] * PAIR + rank)
        lookup.append(jnp.where(present[e], index, spare + entries))

    @pl.loop(0, peers, unroll=2)
    def _(p):
        low = entries
        high = entries
        for e in range(entries):
            high = jnp.where(place[e] == p, e, high)
        for e in reversed(range(entries)):
            low = jnp.where(place[e] == p, e, low)
        chosen[p * PAIR] = low
        chosen[p * PAIR + 1] = high

    inside = slice(PAD, PAD + side)
    for load in loads[7:10]:
        load.wait()
    for s in range(slots):
        m = wet[s].astype(jnp.float32)
        wet_f[s] = m
        md = m * depth[s] * (coupling * 0.5)
        along_md[s, inside] = md
        across_md[s, inside] = md.T

    def await_bytes(ref, sem):
        pltpu.make_async_copy(ref, ref, sem).wait()

    rest = slice(PAD - 1, PAD + side + 1)
    before = slice(PAD - 2, PAD + side)
    after = slice(PAD, PAD + side + 2)
    for t in range(steps):
        out, landing = outs[t], landings[t]
        for s in range(slots):
            surface = terminal[s] if t == 0 else surface_ref[s]
            masked = wet_f[s] * (surface + forces[s])
            along[s, inside] = masked
            across[s, inside] = masked.T
            for at, field, depths in ((0, across, across_md), (2, along, along_md)):
                edges[s * 4 + at, 0:2] = field[s, PAD : PAD + 2]
                edges[s * 4 + at + 1, 0:2] = field[s, PAD + side - 2 : PAD + side]
                if t == 0:
                    edges[s * 4 + at, 2:3] = depths[s, PAD : PAD + 1]
                    edges[s * 4 + at + 1, 2:3] = depths[s, PAD + side - 1 : PAD + side]
        width = 4 if t == 0 else 2
        for start in range(0, spare, 24):
            rows = range(start, min(start + 24, spare))
            picked = [edges[chosen[i], 0:width] for i in rows]
            for i, row in zip(rows, picked):
                out[i] = row
        if t == 0:
            pl.semaphore_wait(barrier, devices - 1)

        def send(shift, there, other):
            at = (0 if shift == basins - 1 else shift + 1) * groups
            landing_at = (2 * groups - at + group) * PAIR
            pltpu.make_async_remote_copy(
                src_ref=out.at[pl.ds((at + other) * PAIR, PAIR)],
                dst_ref=landing.at[pl.ds(landing_at, PAIR)],
                send_sem=send_sem.at[t],
                recv_sem=recv_sem.at[t],
                device_id=(there, other),
                device_id_type=MESH,
            ).start()

        each_peer((1, basins - 1, 0), send)
        for e in range(entries + 1):
            landing[spare + e] = edges[e, 0:width]
        if t + 1 < steps:
            injected(t + 1)
        await_bytes(landing.at[pl.ds(0, (peers - 1) * PAIR)], recv_sem.at[t])
        fetched = [landing[lookup[e]] for e in range(entries)]
        for e in range(entries):
            s, at = e // 4, e % 4
            field, depths = (across, across_md) if at < 2 else (along, along_md)
            got = fetched[e]
            if at % 2 == 0:
                field[s, PAD - 2 : PAD] = got[0:2]
                if t == 0:
                    depths[s, PAD - 1 : PAD] = got[2:3]
            else:
                field[s, PAD + side : PAD + side + 2] = got[0:2]
                if t == 0:
                    depths[s, PAD + side : PAD + side + 1] = got[2:3]
        for s in range(slots):
            for field, depths, flow in (
                (across, across_md, across_flow),
                (along, along_md, along_flow),
            ):
                flow[s, rest] += depths[s, rest] * (field[s, after] - field[s, before])

            def gradient(flow):
                return (coupling * 0.5) * (
                    flow[s, PAD + 1 : PAD + side + 1] - flow[s, PAD - 1 : PAD + side - 1]
                )

            surface_ref[s] = along[s, inside] + (gradient(across_flow).T + gradient(along_flow))

    for load in (loads[1], loads[2], loads[5], loads[6], loads[10]):
        load.wait()
    lanes = sums_out.shape[2]
    row = lax.broadcasted_iota(jnp.int32, (devices, lanes), 0)
    lane = lax.broadcasted_iota(jnp.int32, (devices, lanes), 1)
    number = jnp.where(lane < owned, row * owned + lane, -1)
    shares = jnp.zeros((devices, lanes), jnp.float32)
    for s in range(slots):
        for j in range(patterns):
            down = jnp.sum(basis[s, j] * surface_ref[s], axis=0, keepdims=True)
            partial = jnp.sum(down, axis=1, keepdims=True)
            shares = shares + jnp.where(number == subfault_ref[s, j], partial, 0.0)
    sums_out[...] = shares.reshape(devices, 1, lanes)

    def send_sum(shift, there, other):
        target = there * groups + other
        pltpu.make_async_remote_copy(
            src_ref=sums_out.at[target],
            dst_ref=sums_in.at[me],
            send_sem=sums_sem.at[0],
            recv_sem=sums_sem.at[1],
            device_id=(there, other),
            device_id_type=MESH,
        ).start()

    each_peer([*range(1, basins), 0], send_sum)
    sums_in[me] = sums_out[me]
    source = source_ref[...].reshape(1, owned)
    background = background_ref[...].reshape(1, owned)
    prior = prior_weight * (source - background)
    await_bytes(sums_in.at[pl.ds(0, devices - 1)], sums_sem.at[1])
    mine = jnp.sum(sums_in[...], axis=0)[:, :owned]
    updated_ref[...] = (source - step_ref[0] * (prior + mine)).reshape(owned)
    await_bytes(sums_out.at[pl.ds(0, devices - 1)], sums_sem.at[0])
    for t in range(steps):
        await_bytes(outs[t].at[pl.ds(0, (peers - 1) * PAIR)], send_sem.at[t])


def shards(
    terminal,
    depth,
    wet_cells,
    neighbours,
    gauge_cell,
    misfit,
    basis,
    subfault_index,
    source,
    background,
    step_size,
):
    slots, side, _ = terminal.shape
    steps = misfit.shape[0]
    owned = source.shape[0]
    basins = lax.axis_size("basin")
    groups = lax.axis_size("blk")
    devices = basins * groups
    rows = 3 * groups * PAIR
    entries = slots * 4
    kept = rows + entries + 1
    lanes = -(-owned // 128) * 128
    widths = [4] + [2] * (steps - 1)
    f32 = jnp.float32
    padded = pltpu.VMEM((slots, side + 2 * PAD, side), f32)
    vmem = pl.BlockSpec(memory_space=pltpu.VMEM)
    hbm = pl.BlockSpec(memory_space=pltpu.HBM)
    scalars = (neighbours, subfault_index, step_size)
    vectors = (
        gauge_cell,
        misfit,
        source,
        background,
        terminal,
        wet_cells,
        depth,
        basis,
    )
    operands = scalars + vectors
    return pl.pallas_call(
        functools.partial(kernel, basins, groups),
        out_shape=(
            jax.ShapeDtypeStruct(terminal.shape, f32),
            jax.ShapeDtypeStruct(source.shape, f32),
        ),
        in_specs=[hbm] * len(operands),
        out_specs=(vmem, vmem),
        scratch_shapes=[
            *[pltpu.SMEM(x.shape, x.dtype) for x in scalars],
            *[pltpu.VMEM(x.shape, x.dtype) for x in vectors],
            pltpu.VMEM(terminal.shape, f32),
            pltpu.VMEM(terminal.shape, f32),
            padded,
            padded,
            padded,
            padded,
            padded,
            padded,
            pltpu.VMEM((entries + 1, 4, side), f32),
            pltpu.VMEM((devices, 1, lanes), f32),
            pltpu.VMEM((devices, 1, lanes), f32),
            pltpu.SMEM((rows,), jnp.int32),
            pltpu.SemaphoreType.DMA((len(operands),)),
            pltpu.SemaphoreType.DMA((steps,)),
            pltpu.SemaphoreType.DMA((steps,)),
            pltpu.SemaphoreType.DMA((2,)),
            *[pltpu.VMEM((rows, width, side), f32) for width in widths],
            *[pltpu.VMEM((kept, width, side), f32) for width in widths],
        ],
        compiler_params=pltpu.CompilerParams(
            collective_id=0, has_side_effects=True, vmem_limit_bytes=32 * 1024 * 1024
        ),
        cost_estimate=pl.CostEstimate(flops=4_000_000, bytes_accessed=1_100_000, transcendentals=0),
        name="adjoint",
    )(*operands)


def solution(mesh):
    in_specs = (
        P(("basin", "blk"), None, None),
        P(("basin", "blk"), None, None),
        P(("basin", "blk"), None, None),
        P(("basin", "blk"), None),
        P(("basin", "blk")),
        P(None, ("basin", "blk")),
        P(("basin", "blk"), None, None, None),
        P(("basin", "blk"), None),
        P(("basin", "blk")),
        P(("basin", "blk")),
        P(),
    )
    out_specs = (P(("basin", "blk"), None, None), P(("basin", "blk")))
    return jax.shard_map(shards, mesh=mesh, in_specs=in_specs, out_specs=out_specs, check_vma=False)
```

time: 42.6 us -> 39.5 us (0.927)
  Pallas kernels: 32.8 us -> 30.3 us
  other arithmetic: 0.52 us -> 0 us
    pallas_call x1, Pallas kernels: 32.8 us -> 30.3 us  [shards(): pl.pallas_call(functools.partial(kernel, basins, groups), out_shape=(jax....]
    sub x1 -> x0, other arithmetic: 0.52 us -> none  [shards(): return (surface, source - step_size[0] * gradient)]
    unnamed x21 -> x22, local copies, waits for them, and re-layouts: 7.75 us -> 7.59 us
where the time goes in v2:
time: 39.5 us; the launch traced here: 39.2 us
  Pallas kernels  30.3 us (77%)
  local copies, waits for them, and re-layouts  7.59 us (19%)
  between operations  1.35 us (3%)
    pallas_call x1, Pallas kernels, shards(): pl.pallas_call(functools.partial(kernel, basins, groups), out_shape=(jax....  30.3 us
    unnamed x22, local copies, waits for them, and re-layouts  7.59 us

profile of v2, /device:TPU:0, one launch (start us, length us, event | category | flops | bytes accessed | tf_op | source)
XLA Modules:
  0.0 39.2 jit_solution(4236882646848545234)
XLA Ops:
  0.6 0.0 copy-start.7
  0.6 0.0 copy-start.5
  1.3 0.0 copy-done.7
  1.3 0.0 copy-done.5
  1.3 0.0 copy-start
  1.3 1.0 %copy-done = f32[2,4,128,128]{3,2,1,0:T(8,128)S(1)} copy-done((f32[2,4,128,128]{3,2,1,0:T(8,128)S(1)}, f32[2,4,128,128]{3,2,1,0:T(8,128)}, u32[]{:S(2)}) %copy-start) | copy-done | bytes 524312
  2.4 0.0 copy-start.1
  2.4 0.9 %copy-done.1 = f32[2,128,128]{2,1,0:T(8,128)S(1)} copy-done((f32[2,128,128]{2,1,0:T(8,128)S(1)}, f32[2,128,128]{2,1,0:T(8,128)}, u32[]{:S(2)}) %copy-start.1) | copy-done | bytes 131096
  3.3 0.0 copy-start.2
  3.3 0.9 %copy-done.2 = s32[2,128,128]{2,1,0:T(8,128)S(1)} copy-done((s32[2,128,128]{2,1,0:T(8,128)S(1)}, s32[2,128,128]{2,1,0:T(8,128)}, u32[]{:S(2)}) %copy-start.2) | copy-done | bytes 131096
  4.2 0.0 copy-start.3
  4.2 0.9 %copy-done.3 = f32[2,128,128]{2,1,0:T(8,128)S(1)} copy-done((f32[2,128,128]{2,1,0:T(8,128)S(1)}, f32[2,128,128]{2,1,0:T(8,128)}, u32[]{:S(2)}) %copy-start.3) | copy-done | bytes 131096
  5.1 0.0 copy-start.4
  5.1 0.7 %copy-done.4 = f32[4,32]{1,0:T(4,128)S(1)} copy-done((f32[4,32]{1,0:T(4,128)S(1)}, f32[4,32]{1,0:T(4,128)}, u32[]{:S(2)}) %copy-start.4) | copy-done | bytes 536
  5.8 0.0 copy-start.6
  5.8 0.7 %copy-done.6 = s32[2,4]{1,0:T(2,128)S(1)} copy-done((s32[2,4]{1,0:T(2,128)S(1)}, s32[2,4]{1,0:T(2,128)}, u32[]{:S(2)}) %copy-start.6) | copy-done | bytes 56
  6.5 0.0 copy-start.8
  6.5 0.7 %copy-done.8 = f32[8]{0:T(128)S(1)} copy-done((f32[8]{0:T(128)S(1)}, f32[8]{0:T(128)}, u32[]{:S(2)}) %copy-start.8) | copy-done | bytes 56
  7.1 0.0 copy-start.9
  7.1 0.7 %copy-done.9 = f32[8]{0:T(128)S(1)} copy-done((f32[8]{0:T(128)S(1)}, f32[8]{0:T(128)}, u32[]{:S(2)}) %copy-start.9) | copy-done | bytes 56
  7.8 30.3 %adjoint.1 = (f32[2,128,128]{2,1,0:T(8,128)S(1)}, f32[8]{0:T(128)S(1)}) custom-call(s32[2,4]{1,0:T(2,128)S(1)} %copy-done.5, s32[2,4]{1,0:T(2,128)S(1)} %copy-done.6, f32[1]{0:T(128)S(6)} %copy.15.step_hbm, s32[32]{0:T(128)S(1)} %copy-done.7, f32[4,32]{1,0:T(4,128)S(1)} %copy-done.4, f32[8]{0:T(128)S(1)} %copy-done.8, f32[8]{0:T(128)S(1)} %copy-done.9, ...), custom_call_target="tpu_custom_call" | custom-call | flops 4000000 | bytes 1100000 | tf_op jit(solution)/shard_map/adjoint/pallas_call | solution.py:335
  38.0 0.7 %copy.16 = f32[2,128,128]{2,1,0:T(8,128)} copy(f32[2,128,128]{2,1,0:T(8,128)S(1)} %get-tuple-element.4) | data formatting | bytes 262144
  38.7 0.5 %copy.17 = f32[8]{0:T(128)} copy(f32[8]{0:T(128)S(1)} %get-tuple-element.5) | data formatting | bytes 64
Async XLA Ops:
  0.6 0.7 %copy-start.7 = (s32[32]{0:T(128)S(1)}, s32[32]{0:T(128)}, u32[]{:S(2)}) copy-start(s32[32]{0:T(128)} %gauge_hbm.1) | copy-start | bytes 388
  0.6 0.7 %copy-start.5 = (s32[2,4]{1,0:T(2,128)S(1)}, s32[2,4]{1,0:T(2,128)}, u32[]{:S(2)}) copy-start(s32[2,4]{1,0:T(2,128)} %near_hbm.1) | copy-start | bytes 100
  1.3 1.0 %copy-start = (f32[2,4,128,128]{3,2,1,0:T(8,128)S(1)}, f32[2,4,128,128]{3,2,1,0:T(8,128)}, u32[]{:S(2)}) copy-start(f32[2,4,128,128]{3,2,1,0:T(8,128)} %basis_hbm.1) | copy-start | bytes 1572868
  2.4 0.9 %copy-start.1 = (f32[2,128,128]{2,1,0:T(8,128)S(1)}, f32[2,128,128]{2,1,0:T(8,128)}, u32[]{:S(2)}) copy-start(f32[2,128,128]{2,1,0:T(8,128)} %terminal_hbm.1) | copy-start | bytes 393220
  3.3 0.9 %copy-start.2 = (s32[2,128,128]{2,1,0:T(8,128)S(1)}, s32[2,128,128]{2,1,0:T(8,128)}, u32[]{:S(2)}) copy-start(s32[2,128,128]{2,1,0:T(8,128)} %wet_hbm.1) | copy-start | bytes 393220
  4.2 0.9 %copy-start.3 = (f32[2,128,128]{2,1,0:T(8,128)S(1)}, f32[2,128,128]{2,1,0:T(8,128)}, u32[]{:S(2)}) copy-start(f32[2,128,128]{2,1,0:T(8,128)} %depth_hbm.1) | copy-start | bytes 393220
  5.1 0.7 %copy-start.4 = (f32[4,32]{1,0:T(4,128)S(1)}, f32[4,32]{1,0:T(4,128)}, u32[]{:S(2)}) copy-start(f32[4,32]{1,0:T(4,128)} %misfit_hbm.1) | copy-start | bytes 1540
  5.8 0.7 %copy-start.6 = (s32[2,4]{1,0:T(2,128)S(1)}, s32[2,4]{1,0:T(2,128)}, u32[]{:S(2)}) copy-start(s32[2,4]{1,0:T(2,128)} %subfault_hbm.1) | copy-start | bytes 100
  6.5 0.7 %copy-start.8 = (f32[8]{0:T(128)S(1)}, f32[8]{0:T(128)}, u32[]{:S(2)}) copy-start(f32[8]{0:T(128)} %source_hbm.1) | copy-start | bytes 100
  7.1 0.7 %copy-start.9 = (f32[8]{0:T(128)S(1)}, f32[8]{0:T(128)}, u32[]{:S(2)}) copy-start(f32[8]{0:T(128)} %background_hbm.1) | copy-start | bytes 100

commit v3 on v2

--- a/solution.py
+++ b/solution.py
@@ -39,7 +39,7 @@
     wet_hbm,
     depth_hbm,
     basis_hbm,
-    surface_ref,
+    surface_hbm,
     updated_ref,
     near_ref,
     subfault_ref,
@@ -52,6 +52,7 @@
     wet,
     depth,
     basis,
+    surface_ref,
     wet_f,
     forces,
     across,
@@ -254,6 +255,8 @@
 
             surface_ref[s] = along[s, inside] + (gradient(across_flow).T + gradient(along_flow))
 
+    store = pltpu.make_async_copy(surface_ref, surface_hbm, load_sem.at[len(pairs)])
+    store.start()
     for load in (loads[1], loads[2], loads[5], loads[6], loads[10]):
         load.wait()
     lanes = sums_out.shape[2]
@@ -287,6 +290,7 @@
     await_bytes(sums_in.at[pl.ds(0, devices - 1)], sums_sem.at[1])
     mine = jnp.sum(sums_in[...], axis=0)[:, :owned]
     updated_ref[...] = (source - step_ref[0] * (prior + mine)).reshape(owned)
+    store.wait()
     await_bytes(sums_out.at[pl.ds(0, devices - 1)], sums_sem.at[0])
     for t in range(steps):
         await_bytes(outs[t].at[pl.ds(0, (peers - 1) * PAIR)], send_sem.at[t])
@@ -339,12 +343,13 @@
             jax.ShapeDtypeStruct(source.shape, f32),
         ),
         in_specs=[hbm] * len(operands),
-        out_specs=(vmem, vmem),
+        out_specs=(hbm, vmem),
         scratch_shapes=[
             *[pltpu.SMEM(x.shape, x.dtype) for x in scalars],
             *[pltpu.VMEM(x.shape, x.dtype) for x in vectors],
             pltpu.VMEM(terminal.shape, f32),
             pltpu.VMEM(terminal.shape, f32),
+            pltpu.VMEM(terminal.shape, f32),
             padded,
             padded,
             padded,
@@ -355,7 +360,7 @@
             pltpu.VMEM((devices, 1, lanes), f32),
             pltpu.VMEM((devices, 1, lanes), f32),
             pltpu.SMEM((rows,), jnp.int32),
-            pltpu.SemaphoreType.DMA((len(operands),)),
+            pltpu.SemaphoreType.DMA((len(operands) + 1,)),
             pltpu.SemaphoreType.DMA((steps,)),
             pltpu.SemaphoreType.DMA((steps,)),
             pltpu.SemaphoreType.DMA((2,)),
@@ -363,7 +368,7 @@
             *[pltpu.VMEM((kept, width, side), f32) for width in widths],
         ],
         compiler_params=pltpu.CompilerParams(
-            collective_id=0, has_side_effects=True, vmem_limit_bytes=32 * 1024 * 1024
+            collective_id=0, has_side_effects=True, vmem_limit_bytes=64 * 1024 * 1024
         ),
         cost_estimate=pl.CostEstimate(flops=4_000_000, bytes_accessed=1_100_000, transcendentals=0),
         name="adjoint",

time: 39.5 us -> 33.9 us (0.86)
  local copies, waits for them, and re-layouts: 7.59 us -> 2.08 us
    unnamed x22 -> x4, local copies, waits for them, and re-layouts: 7.59 us -> 2.08 us
where the time goes in v3:
time: 33.9 us; the launch traced here: 33.7 us
  Pallas kernels  30.3 us (89%)
  local copies, waits for them, and re-layouts  2.08 us (6%)
  between operations  1.3 us (4%)
    pallas_call x1, Pallas kernels, shards(): pl.pallas_call(functools.partial(kernel, basins, groups), out_shape=(jax....  30.3 us
    unnamed x4, local copies, waits for them, and re-layouts  2.08 us

profile of v3, /device:TPU:0, one launch (start us, length us, event | category | flops | bytes accessed | tf_op | source)
XLA Modules:
  0.0 33.7 jit_solution(14624861845935369209)
XLA Ops:
  1.3 30.3 %adjoint.1 = (f32[2,128,128]{2,1,0:T(8,128)}, f32[8]{0:T(128)}) custom-call(s32[2,4]{1,0:T(2,128)} %near_hbm.1, s32[2,4]{1,0:T(2,128)} %subfault_hbm.1, f32[1]{0:T(128)S(6)} %copy.15.step_hbm, s32[32]{0:T(128)} %gauge_hbm.1, f32[4,32]{1,0:T(4,128)} %misfit_hbm.1, f32[8]{0:T(128)} %source_hbm.1, f32[8]{0:T(128)} %background_hbm.1, ...), custom_call_target="tpu_custom_call" | custom-call | flops 4000000 | bytes 1100000 | tf_op jit(solution)/shard_map/adjoint/pallas_call | solution.py:339
  31.6 0.0 copy-start
  31.6 1.6 %copy.16 = f32[2,128,128]{2,1,0:T(8,128)} copy(f32[2,128,128]{2,1,0:T(8,128)} %get-tuple-element.4) | data formatting | bytes 262144
  33.2 0.0 copy-done
  33.2 0.5 %copy.17 = f32[8]{0:T(128)} copy(f32[8]{0:T(128)S(1)} %copy-done) | data formatting | bytes 64
Async XLA Ops:
  31.6 1.6 %copy-start = (f32[8]{0:T(128)S(1)}, f32[8]{0:T(128)}, u32[]{:S(2)}) copy-start(f32[8]{0:T(128)} %get-tuple-element.5) | copy-start | bytes 100

commit v4 on v3

--- a/solution.py
+++ b/solution.py
@@ -54,7 +54,14 @@
     basis,
     surface_ref,
     wet_f,
+    wet_t,
     forces,
+    early_across,
+    early_along,
+    late_across,
+    late_along,
+    turned_across,
+    turned_along,
     across,
     along,
     across_md,
@@ -62,6 +69,9 @@
     across_flow,
     along_flow,
     edges,
+    weights,
+    weights_out,
+    weights_in,
     sums_out,
     sums_in,
     chosen,
@@ -115,7 +125,8 @@
 
     each_peer(range(basins), greet)
 
-    for ref in (across_flow, along_flow, edges):
+    zeroed = (across, along, across_md, along_md, across_flow, along_flow, late_across, late_along)
+    for ref in (*zeroed, edges, weights):
         ref[...] = jnp.zeros_like(ref)
 
     loads[3].wait()
@@ -175,115 +186,209 @@
     inside = slice(PAD, PAD + side)
     for load in loads[7:10]:
         load.wait()
+    def await_bytes(ref, sem):
+        pltpu.make_async_copy(ref, ref, sem).wait()
+
     for s in range(slots):
         m = wet[s].astype(jnp.float32)
         wet_f[s] = m
+        wet_t[s] = m.T
         md = m * depth[s] * (coupling * 0.5)
         along_md[s, inside] = md
         across_md[s, inside] = md.T
-
-    def await_bytes(ref, sem):
-        pltpu.make_async_copy(ref, ref, sem).wait()
-
-    rest = slice(PAD - 1, PAD + side + 1)
-    before = slice(PAD - 2, PAD + side)
-    after = slice(PAD, PAD + side + 2)
-    for t in range(steps):
-        out, landing = outs[t], landings[t]
-        for s in range(slots):
-            surface = terminal[s] if t == 0 else surface_ref[s]
-            masked = wet_f[s] * (surface + forces[s])
-            along[s, inside] = masked
-            across[s, inside] = masked.T
-            for at, field, depths in ((0, across, across_md), (2, along, along_md)):
-                edges[s * 4 + at, 0:2] = field[s, PAD : PAD + 2]
-                edges[s * 4 + at + 1, 0:2] = field[s, PAD + side - 2 : PAD + side]
-                if t == 0:
-                    edges[s * 4 + at, 2:3] = depths[s, PAD : PAD + 1]
-                    edges[s * 4 + at + 1, 2:3] = depths[s, PAD + side - 1 : PAD + side]
-        width = 4 if t == 0 else 2
+        masked = m * (terminal[s] + forces[s])
+        along[s, inside] = masked
+        across[s, inside] = masked.T
+
+    ways = (
+        (across, across_md, across_flow, wet_t, early_across, late_across, turned_along),
+        (along, along_md, along_flow, wet_f, early_along, late_along, turned_across),
+    )
+    first, last = PAD, PAD + side - 1
+    half = coupling * 0.5
+    lane_row = lax.broadcasted_iota(jnp.int32, (1, side), 1)
+    for load in (loads[1], loads[10]):
+        load.wait()
+    for s in range(slots):
+        names = jnp.zeros((1, side), jnp.float32)
+        for j in range(patterns):
+            names = jnp.where(lane_row == j, subfault_ref[s, j].astype(jnp.float32), names)
+        for w, (_, depths, *_) in enumerate(ways):
+            low = s * 4 + 2 * w
+            edges[low, 2:3] = depths[s, first : first + 1]
+            edges[low + 1, 2:3] = depths[s, last : last + 1]
+            for e in (low, low + 1):
+                edges[e, 3:4] = names
+
+    def pick(table, out, rows):
         for start in range(0, spare, 24):
-            rows = range(start, min(start + 24, spare))
-            picked = [edges[chosen[i], 0:width] for i in rows]
-            for i, row in zip(rows, picked):
+            span = range(start, min(start + 24, spare))
+            picked = [table[chosen[i], 0:rows] for i in span]
+            for i, row in zip(span, picked):
                 out[i] = row
-        if t == 0:
-            pl.semaphore_wait(barrier, devices - 1)
-
+
+    def keep_own(table, landing, rows):
+        for e in range(entries + 1):
+            landing[spare + e] = table[e, 0:rows]
+
+    def send_all(out, landing, at_sem):
         def send(shift, there, other):
             at = (0 if shift == basins - 1 else shift + 1) * groups
             landing_at = (2 * groups - at + group) * PAIR
             pltpu.make_async_remote_copy(
                 src_ref=out.at[pl.ds((at + other) * PAIR, PAIR)],
                 dst_ref=landing.at[pl.ds(landing_at, PAIR)],
-                send_sem=send_sem.at[t],
-                recv_sem=recv_sem.at[t],
+                send_sem=send_sem.at[at_sem],
+                recv_sem=recv_sem.at[at_sem],
                 device_id=(there, other),
                 device_id_type=MESH,
             ).start()
 
         each_peer((1, basins - 1, 0), send)
-        for e in range(entries + 1):
-            landing[spare + e] = edges[e, 0:width]
+
+    def send_weights():
+        for s in range(slots):
+            for j in range(patterns):
+                upright = basis[s, j]
+                for w, (field, turned) in enumerate(((across_md, upright.T), (along_md, upright))):
+                    low = s * 4 + 2 * w
+                    for e, outer, inner, md_at in (
+                        (low, 0, 1, first),
+                        (low + 1, side - 1, side - 2, last),
+                    ):
+                        near = half * turned[inner : inner + 1] * field[s, md_at : md_at + 1]
+                        weights[e, 2 * j : 2 * j + 1] = near
+                        weights[e, 2 * j + 1 : 2 * j + 2] = half * turned[outer : outer + 1]
+        pick(weights, weights_out, 2 * patterns)
+        send_all(weights_out, weights_in, steps)
+        keep_own(weights, weights_in, 2 * patterns)
+
+    def partial_sums(facing):
+        await_bytes(weights_in.at[pl.ds(0, (peers - 1) * PAIR)], recv_sem.at[steps])
+        lanes = sums_out.shape[2]
+        row = lax.broadcasted_iota(jnp.int32, (devices, lanes), 0)
+        lane = lax.broadcasted_iota(jnp.int32, (devices, lanes), 1)
+        number = jnp.where(lane < owned, row * owned + lane, -1)
+        number_f = number.astype(jnp.float32)
+        shares = jnp.zeros((devices, lanes), jnp.float32)
+        for s in range(slots):
+            for j in range(patterns):
+                down = jnp.sum(basis[s, j] * surface_ref[s], axis=0, keepdims=True)
+                partial = jnp.sum(down, axis=1, keepdims=True)
+                shares = shares + jnp.where(number == subfault_ref[s, j], partial, 0.0)
+        odd = lax.broadcasted_iota(jnp.int32, (2 * patterns, side), 0) % 2 == 1
+        for e in range(entries):
+            near, far = (0, 1) if e % 2 == 0 else (1, 0)
+            near_row = edges[e, near : near + 1]
+            far_row = edges[e, far : far + 1] * edges[e, 2:3]
+            terms = weights_in[lookup[e]] * jnp.where(odd, far_row, near_row)
+            dots = jnp.sum(terms, axis=1, keepdims=True)
+            for j in range(patterns):
+                dot = dots[2 * j : 2 * j + 1] + dots[2 * j + 1 : 2 * j + 2]
+                shares = shares + jnp.where(number_f == facing[e][:, j : j + 1], dot, 0.0)
+        sums_out[...] = shares.reshape(devices, 1, lanes)
+
+    def send_sums():
+        def send_sum(shift, there, other):
+            target = there * groups + other
+            pltpu.make_async_remote_copy(
+                src_ref=sums_out.at[target],
+                dst_ref=sums_in.at[me],
+                send_sem=sums_sem.at[0],
+                recv_sem=sums_sem.at[1],
+                device_id=(there, other),
+                device_id_type=MESH,
+            ).start()
+
+        each_peer([*range(1, basins), 0], send_sum)
+        sums_in[me] = sums_out[me]
+
+    rest = slice(PAD - 1, PAD + side + 1)
+    before = slice(PAD - 2, PAD + side)
+    after = slice(PAD, PAD + side + 2)
+    facing = None
+    for t in range(steps):
+        out, landing = outs[t], landings[t]
+        for s in range(slots):
+            for w, (field, _, _, mask, early, late, turned) in enumerate(ways):
+                for e, at in ((s * 4 + 2 * w, 0), (s * 4 + 2 * w + 1, side - 2)):
+                    if t == 0:
+                        edges[e, 0:2] = field[s, PAD + at : PAD + at + 2]
+                    else:
+                        two = slice(at, at + 2)
+                        edges[e, 0:2] = early[s, two] + mask[s, two] * (
+                            late[s, two] + turned[s, two]
+                        )
+        rows = 4 if t == 0 else 2
+        pick(edges, out, rows)
+        if t == 0:
+            pl.semaphore_wait(barrier, devices - 1)
+        send_all(out, landing, t)
+
+        keep_own(edges, landing, rows)
+        if t == 0:
+            send_weights()
         if t + 1 < steps:
             injected(t + 1)
+        for s in range(slots):
+            for field, depths, flow, mask, early, late, turned in ways:
+                if t > 0:
+                    field[s, inside] = early[s] + mask[s] * (late[s] + turned[s])
+                flow[s, rest] += depths[s, rest] * (field[s, after] - field[s, before])
+
+            def gradient(flow):
+                return half * (
+                    flow[s, PAD + 1 : PAD + side + 1] - flow[s, PAD - 1 : PAD + side - 1]
+                )
+
+            surface = along[s, inside] + (gradient(across_flow).T + gradient(along_flow))
+            if t + 1 < steps:
+                masked = wet_f[s] * (surface + forces[s])
+                early_along[s] = masked
+                early_across[s] = masked.T
+            else:
+                surface_ref[s] = surface
+        if t + 1 == steps:
+            partial_sums(facing)
+            send_sums()
+
         await_bytes(landing.at[pl.ds(0, (peers - 1) * PAIR)], recv_sem.at[t])
         fetched = [landing[lookup[e]] for e in range(entries)]
-        for e in range(entries):
-            s, at = e // 4, e % 4
-            field, depths = (across, across_md) if at < 2 else (along, along_md)
-            got = fetched[e]
-            if at % 2 == 0:
-                field[s, PAD - 2 : PAD] = got[0:2]
+        if t == 0:
+            facing = [got[3:4] for got in fetched]
+        for s in range(slots):
+            for w, (field, depths, flow, mask, early, late, turned) in enumerate(ways):
+                low, high = fetched[s * 4 + 2 * w], fetched[s * 4 + 2 * w + 1]
+                far_low, far_high = -low[0:1], high[1:2]
                 if t == 0:
-                    depths[s, PAD - 1 : PAD] = got[2:3]
+                    depths[s, first - 1 : first] = low[2:3]
+                    depths[s, last + 1 : last + 2] = high[2:3]
+                    far_low = field[s, first : first + 1] + far_low
+                    far_high = far_high - field[s, last : last + 1]
+                far_low = depths[s, first - 1 : first] * far_low
+                near_low = -depths[s, first : first + 1] * low[1:2]
+                near_high = depths[s, last : last + 1] * high[0:1]
+                far_high = depths[s, last + 1 : last + 2] * far_high
+                late[s, 0:1] = -half * far_low
+                late[s, 1:2] = -half * near_low
+                late[s, side - 2 : side - 1] = half * near_high
+                late[s, side - 1 : side] = half * far_high
+                if t + 1 < steps:
+                    flow[s, first - 1 : first] += far_low
+                    flow[s, first : first + 1] += near_low
+                    flow[s, last : last + 1] += near_high
+                    flow[s, last + 1 : last + 2] += far_high
+        for s in range(slots):
+            turned_across[s] = late_across[s].T
+            if t + 1 < steps:
+                turned_along[s] = late_along[s].T
             else:
-                field[s, PAD + side : PAD + side + 2] = got[0:2]
-                if t == 0:
-                    depths[s, PAD + side : PAD + side + 1] = got[2:3]
-        for s in range(slots):
-            for field, depths, flow in (
-                (across, across_md, across_flow),
-                (along, along_md, along_flow),
-            ):
-                flow[s, rest] += depths[s, rest] * (field[s, after] - field[s, before])
-
-            def gradient(flow):
-                return (coupling * 0.5) * (
-                    flow[s, PAD + 1 : PAD + side + 1] - flow[s, PAD - 1 : PAD + side - 1]
-                )
-
-            surface_ref[s] = along[s, inside] + (gradient(across_flow).T + gradient(along_flow))
+                surface_ref[s] += late_along[s] + turned_across[s]
 
     store = pltpu.make_async_copy(surface_ref, surface_hbm, load_sem.at[len(pairs)])
     store.start()
-    for load in (loads[1], loads[2], loads[5], loads[6], loads[10]):
+    for load in (loads[2], loads[5], loads[6]):
         load.wait()
-    lanes = sums_out.shape[2]
-    row = lax.broadcasted_iota(jnp.int32, (devices, lanes), 0)
-    lane = lax.broadcasted_iota(jnp.int32, (devices, lanes), 1)
-    number = jnp.where(lane < owned, row * owned + lane, -1)
-    shares = jnp.zeros((devices, lanes), jnp.float32)
-    for s in range(slots):
-        for j in range(patterns):
-            down = jnp.sum(basis[s, j] * surface_ref[s], axis=0, keepdims=True)
-            partial = jnp.sum(down, axis=1, keepdims=True)
-            shares = shares + jnp.where(number == subfault_ref[s, j], partial, 0.0)
-    sums_out[...] = shares.reshape(devices, 1, lanes)
-
-    def send_sum(shift, there, other):
-        target = there * groups + other
-        pltpu.make_async_remote_copy(
-            src_ref=sums_out.at[target],
-            dst_ref=sums_in.at[me],
-            send_sem=sums_sem.at[0],
-            recv_sem=sums_sem.at[1],
-            device_id=(there, other),
-            device_id_type=MESH,
-        ).start()
-
-    each_peer([*range(1, basins), 0], send_sum)
-    sums_in[me] = sums_out[me]
     source = source_ref[...].reshape(1, owned)
     background = background_ref[...].reshape(1, owned)
     prior = prior_weight * (source - background)
@@ -294,6 +399,7 @@
     await_bytes(sums_out.at[pl.ds(0, devices - 1)], sums_sem.at[0])
     for t in range(steps):
         await_bytes(outs[t].at[pl.ds(0, (peers - 1) * PAIR)], send_sem.at[t])
+    await_bytes(weights_out.at[pl.ds(0, (peers - 1) * PAIR)], send_sem.at[steps])
 
 
 def shards(
@@ -311,6 +417,7 @@
 ):
     slots, side, _ = terminal.shape
     steps = misfit.shape[0]
+    patterns = basis.shape[1]
     owned = source.shape[0]
     basins = lax.axis_size("basin")
     groups = lax.axis_size("blk")
@@ -347,9 +454,7 @@
         scratch_shapes=[
             *[pltpu.SMEM(x.shape, x.dtype) for x in scalars],
             *[pltpu.VMEM(x.shape, x.dtype) for x in vectors],
-            pltpu.VMEM(terminal.shape, f32),
-            pltpu.VMEM(terminal.shape, f32),
-            pltpu.VMEM(terminal.shape, f32),
+            *[pltpu.VMEM(terminal.shape, f32)] * 10,
             padded,
             padded,
             padded,
@@ -357,12 +462,15 @@
             padded,
             padded,
             pltpu.VMEM((entries + 1, 4, side), f32),
+            pltpu.VMEM((entries + 1, 2 * patterns, side), f32),
+            pltpu.VMEM((rows, 2 * patterns, side), f32),
+            pltpu.VMEM((kept, 2 * patterns, side), f32),
             pltpu.VMEM((devices, 1, lanes), f32),
             pltpu.VMEM((devices, 1, lanes), f32),
             pltpu.SMEM((rows,), jnp.int32),
             pltpu.SemaphoreType.DMA((len(operands) + 1,)),
-            pltpu.SemaphoreType.DMA((steps,)),
-            pltpu.SemaphoreType.DMA((steps,)),
+            pltpu.SemaphoreType.DMA((steps + 1,)),
+            pltpu.SemaphoreType.DMA((steps + 1,)),
             pltpu.SemaphoreType.DMA((2,)),
             *[pltpu.VMEM((rows, width, side), f32) for width in widths],
             *[pltpu.VMEM((kept, width, side), f32) for width in widths],

time: 33.9 us -> 31.3 us (0.923)
  Pallas kernels: 30.3 us -> 27.8 us
    pallas_call x1, Pallas kernels: 30.3 us -> 27.8 us  [shards(): pl.pallas_call(functools.partial(kernel, basins, groups), out_shape=(jax....]
where the time goes in v4:
time: 31.3 us; the launch traced here: 31.2 us
  Pallas kernels  27.8 us (89%)
  local copies, waits for them, and re-layouts  2.08 us (7%)
  between operations  1.3 us (4%)
    pallas_call x1, Pallas kernels, shards(): pl.pallas_call(functools.partial(kernel, basins, groups), out_shape=(jax....  27.8 us
    unnamed x4, local copies, waits for them, and re-layouts  2.08 us

profile of v4, /device:TPU:0, one launch (start us, length us, event | category | flops | bytes accessed | tf_op | source)
XLA Modules:
  0.0 31.2 jit_solution(15848099862809631833)
XLA Ops:
  1.3 27.8 %adjoint.1 = (f32[2,128,128]{2,1,0:T(8,128)}, f32[8]{0:T(128)}) custom-call(s32[2,4]{1,0:T(2,128)} %near_hbm.1, s32[2,4]{1,0:T(2,128)} %subfault_hbm.1, f32[1]{0:T(128)S(6)} %copy.15.step_hbm, s32[32]{0:T(128)} %gauge_hbm.1, f32[4,32]{1,0:T(4,128)} %misfit_hbm.1, f32[8]{0:T(128)} %source_hbm.1, f32[8]{0:T(128)} %background_hbm.1, ...), custom_call_target="tpu_custom_call" | custom-call | flops 4000000 | bytes 1100000 | tf_op jit(solution)/shard_map/adjoint/pallas_call | solution.py:446
  29.1 0.0 copy-start
  29.1 1.6 %copy.16 = f32[2,128,128]{2,1,0:T(8,128)} copy(f32[2,128,128]{2,1,0:T(8,128)} %get-tuple-element.4) | data formatting | bytes 262144
  30.7 0.0 copy-done
  30.7 0.5 %copy.17 = f32[8]{0:T(128)} copy(f32[8]{0:T(128)S(1)} %copy-done) | data formatting | bytes 64
Async XLA Ops:
  29.1 1.6 %copy-start = (f32[8]{0:T(128)S(1)}, f32[8]{0:T(128)}, u32[]{:S(2)}) copy-start(f32[8]{0:T(128)} %get-tuple-element.5) | copy-start | bytes 100

commit v5 on v4

--- a/solution.py
+++ b/solution.py
@@ -23,6 +23,12 @@
     left = x - high.astype(jnp.float32)
     middle = left.astype(jnp.bfloat16)
     return high, middle, (left - middle.astype(jnp.float32)).astype(jnp.bfloat16)
+
+
+def weight_plan(steps, patterns):
+    first = min(1, steps - 2)
+    chunks = min(steps - 1 - first, patterns)
+    return first, chunks, -(-patterns // chunks)
 
 
 def kernel(
@@ -70,8 +76,6 @@
     along_flow,
     edges,
     weights,
-    weights_out,
-    weights_in,
     sums_out,
     sums_in,
     chosen,
@@ -83,8 +87,11 @@
 ):
     slots, side, _ = terminal.shape
     steps = misfit_ref.shape[0]
-    outs, landings = halo_buffers[:steps], halo_buffers[steps:]
     patterns = basis.shape[1]
+    first_chunk, chunks, per_chunk = weight_plan(steps, patterns)
+    outs, landings = halo_buffers[:steps], halo_buffers[steps : 2 * steps]
+    weights_out = halo_buffers[2 * steps : 2 * steps + chunks]
+    weights_in = halo_buffers[2 * steps + chunks :]
     owned = source_ref.shape[0]
     entries = slots * 4
     devices = basins * groups
@@ -246,9 +253,10 @@
 
         each_peer((1, basins - 1, 0), send)
 
-    def send_weights():
+    def send_weights(c):
+        own = range(c * per_chunk, min((c + 1) * per_chunk, patterns))
         for s in range(slots):
-            for j in range(patterns):
+            for i, j in enumerate(own):
                 upright = basis[s, j]
                 for w, (field, turned) in enumerate(((across_md, upright.T), (along_md, upright))):
                     low = s * 4 + 2 * w
@@ -257,14 +265,15 @@
                         (low + 1, side - 1, side - 2, last),
                     ):
                         near = half * turned[inner : inner + 1] * field[s, md_at : md_at + 1]
-                        weights[e, 2 * j : 2 * j + 1] = near
-                        weights[e, 2 * j + 1 : 2 * j + 2] = half * turned[outer : outer + 1]
-        pick(weights, weights_out, 2 * patterns)
-        send_all(weights_out, weights_in, steps)
-        keep_own(weights, weights_in, 2 * patterns)
+                        weights[c, e, 2 * i : 2 * i + 1] = near
+                        weights[c, e, 2 * i + 1 : 2 * i + 2] = half * turned[outer : outer + 1]
+        pick(weights.at[c], weights_out[c], 2 * per_chunk)
+        send_all(weights_out[c], weights_in[c], steps + c)
+        keep_own(weights.at[c], weights_in[c], 2 * per_chunk)
 
     def partial_sums(facing):
-        await_bytes(weights_in.at[pl.ds(0, (peers - 1) * PAIR)], recv_sem.at[steps])
+        for c in range(chunks):
+            await_bytes(weights_in[c].at[pl.ds(0, (peers - 1) * PAIR)], recv_sem.at[steps + c])
         lanes = sums_out.shape[2]
         row = lax.broadcasted_iota(jnp.int32, (devices, lanes), 0)
         lane = lax.broadcasted_iota(jnp.int32, (devices, lanes), 1)
@@ -276,16 +285,17 @@
                 down = jnp.sum(basis[s, j] * surface_ref[s], axis=0, keepdims=True)
                 partial = jnp.sum(down, axis=1, keepdims=True)
                 shares = shares + jnp.where(number == subfault_ref[s, j], partial, 0.0)
-        odd = lax.broadcasted_iota(jnp.int32, (2 * patterns, side), 0) % 2 == 1
+        odd = lax.broadcasted_iota(jnp.int32, (2 * per_chunk, side), 0) % 2 == 1
         for e in range(entries):
             near, far = (0, 1) if e % 2 == 0 else (1, 0)
             near_row = edges[e, near : near + 1]
             far_row = edges[e, far : far + 1] * edges[e, 2:3]
-            terms = weights_in[lookup[e]] * jnp.where(odd, far_row, near_row)
-            dots = jnp.sum(terms, axis=1, keepdims=True)
-            for j in range(patterns):
-                dot = dots[2 * j : 2 * j + 1] + dots[2 * j + 1 : 2 * j + 2]
-                shares = shares + jnp.where(number_f == facing[e][:, j : j + 1], dot, 0.0)
+            for c in range(chunks):
+                terms = weights_in[c][lookup[e]] * jnp.where(odd, far_row, near_row)
+                dots = jnp.sum(terms, axis=1, keepdims=True)
+                for i, j in enumerate(range(c * per_chunk, min((c + 1) * per_chunk, patterns))):
+                    dot = dots[2 * i : 2 * i + 1] + dots[2 * i + 1 : 2 * i + 2]
+                    shares = shares + jnp.where(number_f == facing[e][:, j : j + 1], dot, 0.0)
         sums_out[...] = shares.reshape(devices, 1, lanes)
 
     def send_sums():
@@ -326,8 +336,8 @@
         send_all(out, landing, t)
 
         keep_own(edges, landing, rows)
-        if t == 0:
-            send_weights()
+        if first_chunk <= t < first_chunk + chunks:
+            send_weights(t - first_chunk)
         if t + 1 < steps:
             injected(t + 1)
         for s in range(slots):
@@ -399,7 +409,17 @@
     await_bytes(sums_out.at[pl.ds(0, devices - 1)], sums_sem.at[0])
     for t in range(steps):
         await_bytes(outs[t].at[pl.ds(0, (peers - 1) * PAIR)], send_sem.at[t])
-    await_bytes(weights_out.at[pl.ds(0, (peers - 1) * PAIR)], send_sem.at[steps])
+    for c in range(chunks):
+        await_bytes(weights_out[c].at[pl.ds(0, (peers - 1) * PAIR)], send_sem.at[steps + c])
+
+
+def hand_over(surface, updated, surface_out, updated_out, sem):
+    first = pltpu.make_async_copy(surface, surface_out, sem.at[0])
+    second = pltpu.make_async_copy(updated, updated_out, sem.at[1])
+    first.start()
+    second.start()
+    first.wait()
+    second.wait()
 
 
 def shards(
@@ -418,6 +438,7 @@
     slots, side, _ = terminal.shape
     steps = misfit.shape[0]
     patterns = basis.shape[1]
+    first_chunk, chunks, per_chunk = weight_plan(steps, patterns)
     owned = source.shape[0]
     basins = lax.axis_size("basin")
     groups = lax.axis_size("blk")
@@ -443,7 +464,7 @@
         basis,
     )
     operands = scalars + vectors
-    return pl.pallas_call(
+    results = pl.pallas_call(
         functools.partial(kernel, basins, groups),
         out_shape=(
             jax.ShapeDtypeStruct(terminal.shape, f32),
@@ -462,18 +483,18 @@
             padded,
             padded,
             pltpu.VMEM((entries + 1, 4, side), f32),
-            pltpu.VMEM((entries + 1, 2 * patterns, side), f32),
-            pltpu.VMEM((rows, 2 * patterns, side), f32),
-            pltpu.VMEM((kept, 2 * patterns, side), f32),
+            pltpu.VMEM((chunks, entries + 1, 2 * per_chunk, side), f32),
             pltpu.VMEM((devices, 1, lanes), f32),
             pltpu.VMEM((devices, 1, lanes), f32),
             pltpu.SMEM((rows,), jnp.int32),
             pltpu.SemaphoreType.DMA((len(operands) + 1,)),
-            pltpu.SemaphoreType.DMA((steps + 1,)),
-            pltpu.SemaphoreType.DMA((steps + 1,)),
+            pltpu.SemaphoreType.DMA((steps + chunks,)),
+            pltpu.SemaphoreType.DMA((steps + chunks,)),
             pltpu.SemaphoreType.DMA((2,)),
             *[pltpu.VMEM((rows, width, side), f32) for width in widths],
             *[pltpu.VMEM((kept, width, side), f32) for width in widths],
+            *[pltpu.VMEM((rows, 2 * per_chunk, side), f32)] * chunks,
+            *[pltpu.VMEM((kept, 2 * per_chunk, side), f32)] * chunks,
         ],
         compiler_params=pltpu.CompilerParams(
             collective_id=0, has_side_effects=True, vmem_limit_bytes=64 * 1024 * 1024
@@ -481,6 +502,15 @@
         cost_estimate=pl.CostEstimate(flops=4_000_000, bytes_accessed=1_100_000, transcendentals=0),
         name="adjoint",
     )(*operands)
+    return pl.pallas_call(
+        hand_over,
+        out_shape=tuple(jax.ShapeDtypeStruct(x.shape, x.dtype) for x in results),
+        in_specs=[hbm] * 2,
+        out_specs=(hbm, hbm),
+        scratch_shapes=[pltpu.SemaphoreType.DMA((2,))],
+        compiler_params=pltpu.CompilerParams(vmem_limit_bytes=64 * 1024 * 1024),
+        name="hand_over",
+    )(*results)
 
 
 def solution(mesh):

time: 31.3 us -> 34.9 us (1.12)
  Pallas kernels: 27.8 us -> 33.4 us
  local copies, waits for them, and re-layouts: 2.08 us -> 0 us
    pallas_call x0 -> x1, Pallas kernels: none -> 5.11 us  [shards(): pl.pallas_call(hand_over, out_shape=tuple((jax.ShapeDtypeStruct(x.shape,...]
    unnamed x4 -> x0, local copies, waits for them, and re-layouts: 2.08 us -> none
    pallas_call x1, Pallas kernels: 27.8 us -> 28.3 us  [shards(): pl.pallas_call(functools.partial(kernel, basins, groups), out_shape=(jax....]
where the time goes in v5:
time: 34.9 us; the launch traced here: 34.7 us
  Pallas kernels  33.4 us (96%)
  between operations  1.29 us (4%)
    pallas_call x1, Pallas kernels, shards(): pl.pallas_call(functools.partial(kernel, basins, groups), out_shape=(jax....  28.3 us
    pallas_call x1, Pallas kernels, shards(): pl.pallas_call(hand_over, out_shape=tuple((jax.ShapeDtypeStruct(x.shape,...  5.11 us

profile of v5, /device:TPU:0, one launch (start us, length us, event | category | flops | bytes accessed | tf_op | source)
XLA Modules:
  0.0 34.7 jit_solution(9871772709369641730)
XLA Ops:
  1.3 28.3 %adjoint.1 = (f32[2,128,128]{2,1,0:T(8,128)}, f32[8]{0:T(128)}) custom-call(s32[2,4]{1,0:T(2,128)} %near_hbm.1, s32[2,4]{1,0:T(2,128)} %subfault_hbm.1, f32[1]{0:T(128)S(6)} %copy.13.step_hbm, s32[32]{0:T(128)} %gauge_hbm.1, f32[4,32]{1,0:T(4,128)} %misfit_hbm.1, f32[8]{0:T(128)} %source_hbm.1, f32[8]{0:T(128)} %background_hbm.1, ...), custom_call_target="tpu_custom_call" | custom-call | flops 4000000 | bytes 1100000 | tf_op jit(solution)/shard_map/adjoint/pallas_call | solution.py:467
  29.6 5.1 %hand_over.1 = (f32[2,128,128]{2,1,0:T(8,128)}, f32[8]{0:T(128)}) custom-call(f32[2,128,128]{2,1,0:T(8,128)} %get-tuple-element.4.surface, f32[8]{0:T(128)} %get-tuple-element.5.updated), custom_call_target="tpu_custom_call" | custom-call | tf_op jit(solution)/shard_map/hand_over/pallas_call | solution.py:505

commit v6 on v5

--- a/solution.py
+++ b/solution.py
@@ -11,6 +11,7 @@
 prior_weight = 0.5
 MESH = pl.DeviceIdType.MESH
 PAD = 8
+PIECES = 4
 PAIR = 2
 
 
@@ -26,8 +27,8 @@
 
 
 def weight_plan(steps, patterns):
-    first = min(1, steps - 2)
-    chunks = min(steps - 1 - first, patterns)
+    first = 0
+    chunks = 1
     return first, chunks, -(-patterns // chunks)
 
 
@@ -317,6 +318,8 @@
     before = slice(PAD - 2, PAD + side)
     after = slice(PAD, PAD + side + 2)
     facing = None
+    outer_lanes = (0, 1, side - 2, side - 1)
+    late_rows = {}
     for t in range(steps):
         out, landing = outs[t], landings[t]
         for s in range(slots):
@@ -325,10 +328,15 @@
                     if t == 0:
                         edges[e, 0:2] = field[s, PAD + at : PAD + at + 2]
                     else:
-                        two = slice(at, at + 2)
-                        edges[e, 0:2] = early[s, two] + mask[s, two] * (
-                            late[s, two] + turned[s, two]
-                        )
+                        for r in range(2):
+                            y = at + r
+                            own = late_rows[s, w][outer_lanes.index(y)]
+                            crossing = jnp.zeros_like(own)
+                            for x, other in zip(outer_lanes, late_rows[s, 1 - w]):
+                                crossing = jnp.where(lane_row == x, other[:, y : y + 1], crossing)
+                            edges[e, r : r + 1] = early[s, y : y + 1] + mask[s, y : y + 1] * (
+                                own + crossing
+                            )
         rows = 4 if t == 0 else 2
         pick(edges, out, rows)
         if t == 0:
@@ -341,6 +349,9 @@
         if t + 1 < steps:
             injected(t + 1)
         for s in range(slots):
+            if t > 0:
+                turned_across[s] = late_across[s].T
+                turned_along[s] = late_along[s].T
             for field, depths, flow, mask, early, late, turned in ways:
                 if t > 0:
                     field[s, inside] = early[s] + mask[s] * (late[s] + turned[s])
@@ -379,22 +390,22 @@
                 near_low = -depths[s, first : first + 1] * low[1:2]
                 near_high = depths[s, last : last + 1] * high[0:1]
                 far_high = depths[s, last + 1 : last + 2] * far_high
-                late[s, 0:1] = -half * far_low
-                late[s, 1:2] = -half * near_low
-                late[s, side - 2 : side - 1] = half * near_high
-                late[s, side - 1 : side] = half * far_high
+                late_rows[s, w] = (
+                    -half * far_low,
+                    -half * near_low,
+                    half * near_high,
+                    half * far_high,
+                )
+                for y, late_row in zip(outer_lanes, late_rows[s, w]):
+                    late[s, y : y + 1] = late_row
                 if t + 1 < steps:
                     flow[s, first - 1 : first] += far_low
                     flow[s, first : first + 1] += near_low
                     flow[s, last : last + 1] += near_high
                     flow[s, last + 1 : last + 2] += far_high
-        for s in range(slots):
-            turned_across[s] = late_across[s].T
-            if t + 1 < steps:
-                turned_along[s] = late_along[s].T
-            else:
-                surface_ref[s] += late_along[s] + turned_across[s]
-
+
+    for s in range(slots):
+        surface_ref[s] += late_along[s] + late_across[s].T
     store = pltpu.make_async_copy(surface_ref, surface_hbm, load_sem.at[len(pairs)])
     store.start()
     for load in (loads[2], loads[5], loads[6]):
@@ -413,13 +424,23 @@
         await_bytes(weights_out[c].at[pl.ds(0, (peers - 1) * PAIR)], send_sem.at[steps + c])
 
 
-def hand_over(surface, updated, surface_out, updated_out, sem):
-    first = pltpu.make_async_copy(surface, surface_out, sem.at[0])
-    second = pltpu.make_async_copy(updated, updated_out, sem.at[1])
-    first.start()
-    second.start()
-    first.wait()
-    second.wait()
+def hand_over(surface, updated, surface_out, updated_out, surface_held, updated_held, sem):
+    slots, side, _ = surface.shape
+    size = side // PIECES
+    moves = [(updated, updated_held, updated_out)]
+    for s in range(slots):
+        for i in range(PIECES):
+            part = (s, pl.ds(i * size, size))
+            moves.append((surface.at[part], surface_held.at[part], surface_out.at[part]))
+    ins = [pltpu.make_async_copy(a, b, sem.at[0, i]) for i, (a, b, _) in enumerate(moves)]
+    outs = [pltpu.make_async_copy(b, c, sem.at[1, i]) for i, (_, b, c) in enumerate(moves)]
+    for copy in ins:
+        copy.start()
+    for arrived, copy in zip(ins, outs):
+        arrived.wait()
+        copy.start()
+    for copy in outs:
+        copy.wait()
 
 
 def shards(
@@ -507,7 +528,10 @@
         out_shape=tuple(jax.ShapeDtypeStruct(x.shape, x.dtype) for x in results),
         in_specs=[hbm] * 2,
         out_specs=(hbm, hbm),
-        scratch_shapes=[pltpu.SemaphoreType.DMA((2,))],
+        scratch_shapes=[
+            *[pltpu.VMEM(x.shape, x.dtype) for x in results],
+            pltpu.SemaphoreType.DMA((2, slots * PIECES + 1)),
+        ],
         compiler_params=pltpu.CompilerParams(vmem_limit_bytes=64 * 1024 * 1024),
         name="hand_over",
     )(*results)

time: 34.9 us -> 31 us (0.89)
  Pallas kernels: 33.4 us -> 29.5 us
    pallas_call x1, Pallas kernels: 5.11 us -> 1.6 us  [shards(): pl.pallas_call(hand_over, out_shape=tuple((jax.ShapeDtypeStruct(x.shape,...]
    pallas_call x1, Pallas kernels: 28.3 us -> 27.9 us  [shards(): pl.pallas_call(functools.partial(kernel, basins, groups), out_shape=(jax....]
where the time goes in v6:
time: 31 us; the launch traced here: 30.8 us
  Pallas kernels  29.5 us (95%)
  between operations  1.29 us (4%)
    pallas_call x1, Pallas kernels, shards(): pl.pallas_call(functools.partial(kernel, basins, groups), out_shape=(jax....  27.9 us
    pallas_call x1, Pallas kernels, shards(): pl.pallas_call(hand_over, out_shape=tuple((jax.ShapeDtypeStruct(x.shape,...  1.6 us

profile of v6, /device:TPU:0, one launch (start us, length us, event | category | flops | bytes accessed | tf_op | source)
XLA Modules:
  0.0 30.8 jit_solution(3818074225769102596)
XLA Ops:
  1.3 27.9 %adjoint.1 = (f32[2,128,128]{2,1,0:T(8,128)}, f32[8]{0:T(128)}) custom-call(s32[2,4]{1,0:T(2,128)} %near_hbm.1, s32[2,4]{1,0:T(2,128)} %subfault_hbm.1, f32[1]{0:T(128)S(6)} %copy.13.step_hbm, s32[32]{0:T(128)} %gauge_hbm.1, f32[4,32]{1,0:T(4,128)} %misfit_hbm.1, f32[8]{0:T(128)} %source_hbm.1, f32[8]{0:T(128)} %background_hbm.1, ...), custom_call_target="tpu_custom_call" | custom-call | flops 4000000 | bytes 1100000 | tf_op jit(solution)/shard_map/adjoint/pallas_call | solution.py:488
  29.2 1.6 %hand_over.1 = (f32[2,128,128]{2,1,0:T(8,128)}, f32[8]{0:T(128)}) custom-call(f32[2,128,128]{2,1,0:T(8,128)} %get-tuple-element.4.surface, f32[8]{0:T(128)} %get-tuple-element.5.updated), custom_call_target="tpu_custom_call" | custom-call | tf_op jit(solution)/shard_map/hand_over/pallas_call | solution.py:526

commit v7 on v6

--- a/solution.py
+++ b/solution.py
@@ -133,9 +133,7 @@
 
     each_peer(range(basins), greet)
 
-    zeroed = (across, along, across_md, along_md, across_flow, along_flow, late_across, late_along)
-    for ref in (*zeroed, edges, weights):
-        ref[...] = jnp.zeros_like(ref)
+    edges[...] = jnp.zeros_like(edges)
 
     loads[3].wait()
     loads[4].wait()
@@ -170,17 +168,7 @@
         jnp.where(present[e], heading[e] * groups + holder[e] % groups, -1)
         for e in range(entries)
     ]
-    lookup = []
-    for e in range(entries):
-        rank = 0
-        for f in range(entries):
-            if f != e:
-                earlier = (place[f] == place[e]) & (origin[f] < origin[e])
-                rank = jnp.where(earlier, 1, rank)
-        index = jnp.where(local[e], spare + origin[e], place[e] * PAIR + rank)
-        lookup.append(jnp.where(present[e], index, spare + entries))
-
-    @pl.loop(0, peers, unroll=2)
+    @pl.loop(0, peers, unroll=8)
     def _(p):
         low = entries
         high = entries
@@ -200,7 +188,6 @@
     for s in range(slots):
         m = wet[s].astype(jnp.float32)
         wet_f[s] = m
-        wet_t[s] = m.T
         md = m * depth[s] * (coupling * 0.5)
         along_md[s, inside] = md
         across_md[s, inside] = md.T
@@ -215,8 +202,7 @@
     first, last = PAD, PAD + side - 1
     half = coupling * 0.5
     lane_row = lax.broadcasted_iota(jnp.int32, (1, side), 1)
-    for load in (loads[1], loads[10]):
-        load.wait()
+    loads[1].wait()
     for s in range(slots):
         names = jnp.zeros((1, side), jnp.float32)
         for j in range(patterns):
@@ -344,6 +330,24 @@
         send_all(out, landing, t)
 
         keep_own(edges, landing, rows)
+        if t == 0:
+            for ref in (across_flow, along_flow, late_across, late_along, weights):
+                ref[...] = jnp.zeros_like(ref)
+            for s in range(slots):
+                wet_t[s] = wet_f[s].T
+                for ref in (across, along, across_md, along_md):
+                    ref[s, :PAD] = jnp.zeros((PAD, side), jnp.float32)
+                    ref[s, PAD + side :] = jnp.zeros((PAD, side), jnp.float32)
+            lookup = []
+            for e in range(entries):
+                rank = 0
+                for f in range(entries):
+                    if f != e:
+                        earlier = (place[f] == place[e]) & (origin[f] < origin[e])
+                        rank = jnp.where(earlier, 1, rank)
+                index = jnp.where(local[e], spare + origin[e], place[e] * PAIR + rank)
+                lookup.append(jnp.where(present[e], index, spare + entries))
+            loads[10].wait()
         if first_chunk <= t < first_chunk + chunks:
             send_weights(t - first_chunk)
         if t + 1 < steps:

time: 31 us -> 31 us (level)
  no operation moved by 1% of the time
where the time goes in v7:
time: 31 us; the launch traced here: 30.8 us
  Pallas kernels  29.5 us (95%)
  between operations  1.29 us (4%)
    pallas_call x1, Pallas kernels, shards(): pl.pallas_call(functools.partial(kernel, basins, groups), out_shape=(jax....  27.9 us
    pallas_call x1, Pallas kernels, shards(): pl.pallas_call(hand_over, out_shape=tuple((jax.ShapeDtypeStruct(x.shape,...  1.6 us

profile of v7, /device:TPU:0, one launch (start us, length us, event | category | flops | bytes accessed | tf_op | source)
XLA Modules:
  0.0 30.8 jit_solution(6479858571494705433)
XLA Ops:
  1.3 27.9 %adjoint.1 = (f32[2,128,128]{2,1,0:T(8,128)}, f32[8]{0:T(128)}) custom-call(s32[2,4]{1,0:T(2,128)} %near_hbm.1, s32[2,4]{1,0:T(2,128)} %subfault_hbm.1, f32[1]{0:T(128)S(6)} %copy.13.step_hbm, s32[32]{0:T(128)} %gauge_hbm.1, f32[4,32]{1,0:T(4,128)} %misfit_hbm.1, f32[8]{0:T(128)} %source_hbm.1, f32[8]{0:T(128)} %background_hbm.1, ...), custom_call_target="tpu_custom_call" | custom-call | flops 4000000 | bytes 1100000 | tf_op jit(solution)/shard_map/adjoint/pallas_call | solution.py:492
  29.2 1.6 %hand_over.1 = (f32[2,128,128]{2,1,0:T(8,128)}, f32[8]{0:T(128)}) custom-call(f32[2,128,128]{2,1,0:T(8,128)} %get-tuple-element.4.surface, f32[8]{0:T(128)} %get-tuple-element.5.updated), custom_call_target="tpu_custom_call" | custom-call | tf_op jit(solution)/shard_map/hand_over/pallas_call | solution.py:530

commit v8 on v7

--- a/solution.py
+++ b/solution.py
@@ -115,9 +115,6 @@
         (basis_hbm, basis),
     )
     loads = [pltpu.make_async_copy(a, b, load_sem.at[i]) for i, (a, b) in enumerate(pairs)]
-    for load in loads:
-        load.start()
-
     def each_peer(shifts, body):
         for shift in shifts:
             there = wrapped(basin + shift, basins)
@@ -132,6 +129,8 @@
         pl.semaphore_signal(barrier, inc=1, device_id=(there, other), device_id_type=MESH)
 
     each_peer(range(basins), greet)
+    for load in loads:
+        load.start()
 
     edges[...] = jnp.zeros_like(edges)
 
@@ -258,20 +257,13 @@
         send_all(weights_out[c], weights_in[c], steps + c)
         keep_own(weights.at[c], weights_in[c], 2 * per_chunk)
 
-    def partial_sums(facing):
-        for c in range(chunks):
-            await_bytes(weights_in[c].at[pl.ds(0, (peers - 1) * PAIR)], recv_sem.at[steps + c])
+    def halo_sums(facing):
         lanes = sums_out.shape[2]
         row = lax.broadcasted_iota(jnp.int32, (devices, lanes), 0)
         lane = lax.broadcasted_iota(jnp.int32, (devices, lanes), 1)
         number = jnp.where(lane < owned, row * owned + lane, -1)
         number_f = number.astype(jnp.float32)
         shares = jnp.zeros((devices, lanes), jnp.float32)
-        for s in range(slots):
-            for j in range(patterns):
-                down = jnp.sum(basis[s, j] * surface_ref[s], axis=0, keepdims=True)
-                partial = jnp.sum(down, axis=1, keepdims=True)
-                shares = shares + jnp.where(number == subfault_ref[s, j], partial, 0.0)
         odd = lax.broadcasted_iota(jnp.int32, (2 * per_chunk, side), 0) % 2 == 1
         for e in range(entries):
             near, far = (0, 1) if e % 2 == 0 else (1, 0)
@@ -283,7 +275,15 @@
                 for i, j in enumerate(range(c * per_chunk, min((c + 1) * per_chunk, patterns))):
                     dot = dots[2 * i : 2 * i + 1] + dots[2 * i + 1 : 2 * i + 2]
                     shares = shares + jnp.where(number_f == facing[e][:, j : j + 1], dot, 0.0)
-        sums_out[...] = shares.reshape(devices, 1, lanes)
+        return number, shares
+
+    def partial_sums(number, shares):
+        for s in range(slots):
+            for j in range(patterns):
+                down = jnp.sum(basis[s, j] * surface_ref[s], axis=0, keepdims=True)
+                partial = jnp.sum(down, axis=1, keepdims=True)
+                shares = shares + jnp.where(number == subfault_ref[s, j], partial, 0.0)
+        sums_out[...] = shares.reshape(sums_out.shape)
 
     def send_sums():
         def send_sum(shift, there, other):
@@ -325,6 +325,10 @@
                             )
         rows = 4 if t == 0 else 2
         pick(edges, out, rows)
+        if t + 1 == steps:
+            for c in range(chunks):
+                landed = weights_in[c].at[pl.ds(0, (peers - 1) * PAIR)]
+                await_bytes(landed, recv_sem.at[steps + c])
         if t == 0:
             pl.semaphore_wait(barrier, devices - 1)
         send_all(out, landing, t)
@@ -352,6 +356,8 @@
             send_weights(t - first_chunk)
         if t + 1 < steps:
             injected(t + 1)
+        else:
+            crossing_sums = halo_sums(facing)
         for s in range(slots):
             if t > 0:
                 turned_across[s] = late_across[s].T
@@ -374,7 +380,7 @@
             else:
                 surface_ref[s] = surface
         if t + 1 == steps:
-            partial_sums(facing)
+            partial_sums(*crossing_sums)
             send_sums()
 
         await_bytes(landing.at[pl.ds(0, (peers - 1) * PAIR)], recv_sem.at[t])

time: 31 us -> 31 us (level)
  no operation moved by 1% of the time
where the time goes in v8:
time: 31 us; the launch traced here: 30.8 us
  Pallas kernels  29.5 us (95%)
  between operations  1.29 us (4%)
    pallas_call x1, Pallas kernels, shards(): pl.pallas_call(functools.partial(kernel, basins, groups), out_shape=(jax....  27.9 us
    pallas_call x1, Pallas kernels, shards(): pl.pallas_call(hand_over, out_shape=tuple((jax.ShapeDtypeStruct(x.shape,...  1.6 us

profile of v8, /device:TPU:0, one launch (start us, length us, event | category | flops | bytes accessed | tf_op | source)
XLA Modules:
  0.0 30.8 jit_solution(12652192008116823349)
XLA Ops:
  1.3 27.9 %adjoint.1 = (f32[2,128,128]{2,1,0:T(8,128)}, f32[8]{0:T(128)}) custom-call(s32[2,4]{1,0:T(2,128)} %near_hbm.1, s32[2,4]{1,0:T(2,128)} %subfault_hbm.1, f32[1]{0:T(128)S(6)} %copy.13.step_hbm, s32[32]{0:T(128)} %gauge_hbm.1, f32[4,32]{1,0:T(4,128)} %misfit_hbm.1, f32[8]{0:T(128)} %source_hbm.1, f32[8]{0:T(128)} %background_hbm.1, ...), custom_call_target="tpu_custom_call" | custom-call | flops 4000000 | bytes 1100000 | tf_op jit(solution)/shard_map/adjoint/pallas_call | solution.py:498
  29.2 1.6 %hand_over.1 = (f32[2,128,128]{2,1,0:T(8,128)}, f32[8]{0:T(128)}) custom-call(f32[2,128,128]{2,1,0:T(8,128)} %get-tuple-element.4.surface, f32[8]{0:T(128)} %get-tuple-element.5.updated), custom_call_target="tpu_custom_call" | custom-call | tf_op jit(solution)/shard_map/hand_over/pallas_call | solution.py:536

commit v9 on v7

--- a/solution.py
+++ b/solution.py
@@ -214,9 +214,9 @@
             for e in (low, low + 1):
                 edges[e, 3:4] = names
 
-    def pick(table, out, rows):
-        for start in range(0, spare, 24):
-            span = range(start, min(start + 24, spare))
+    def pick(table, out, rows, low, high):
+        for start in range(low, high, 24):
+            span = range(start, min(start + 24, high))
             picked = [table[chosen[i], 0:rows] for i in span]
             for i, row in zip(span, picked):
                 out[i] = row
@@ -225,7 +225,7 @@
         for e in range(entries + 1):
             landing[spare + e] = table[e, 0:rows]
 
-    def send_all(out, landing, at_sem):
+    def send_all(table, rows, out, landing, at_sem):
         def send(shift, there, other):
             at = (0 if shift == basins - 1 else shift + 1) * groups
             landing_at = (2 * groups - at + group) * PAIR
@@ -238,7 +238,9 @@
                 device_id_type=MESH,
             ).start()
 
-        each_peer((1, basins - 1, 0), send)
+        for shift, at in ((1, 2 * groups), (basins - 1, 0), (0, groups)):
+            pick(table, out, rows, at * PAIR, (at + groups) * PAIR)
+            each_peer((shift,), send)
 
     def send_weights(c):
         own = range(c * per_chunk, min((c + 1) * per_chunk, patterns))
@@ -254,8 +256,7 @@
                         near = half * turned[inner : inner + 1] * field[s, md_at : md_at + 1]
                         weights[c, e, 2 * i : 2 * i + 1] = near
                         weights[c, e, 2 * i + 1 : 2 * i + 2] = half * turned[outer : outer + 1]
-        pick(weights.at[c], weights_out[c], 2 * per_chunk)
-        send_all(weights_out[c], weights_in[c], steps + c)
+        send_all(weights.at[c], 2 * per_chunk, weights_out[c], weights_in[c], steps + c)
         keep_own(weights.at[c], weights_in[c], 2 * per_chunk)
 
     def partial_sums(facing):
@@ -324,10 +325,9 @@
                                 own + crossing
                             )
         rows = 4 if t == 0 else 2
-        pick(edges, out, rows)
         if t == 0:
             pl.semaphore_wait(barrier, devices - 1)
-        send_all(out, landing, t)
+        send_all(edges, rows, out, landing, t)
 
         keep_own(edges, landing, rows)
         if t == 0:

time: 31 us -> 31 us (level)
  no operation moved by 1% of the time
where the time goes in v9:
time: 31 us; the launch traced here: 30.8 us
  Pallas kernels  29.5 us (95%)
  between operations  1.29 us (4%)
    pallas_call x1, Pallas kernels, shards(): pl.pallas_call(functools.partial(kernel, basins, groups), out_shape=(jax....  27.9 us
    pallas_call x1, Pallas kernels, shards(): pl.pallas_call(hand_over, out_shape=tuple((jax.ShapeDtypeStruct(x.shape,...  1.6 us

profile of v9, /device:TPU:0, one launch (start us, length us, event | category | flops | bytes accessed | tf_op | source)
XLA Modules:
  0.0 30.8 jit_solution(14731816780475931406)
XLA Ops:
  1.3 27.9 %adjoint.1 = (f32[2,128,128]{2,1,0:T(8,128)}, f32[8]{0:T(128)}) custom-call(s32[2,4]{1,0:T(2,128)} %near_hbm.1, s32[2,4]{1,0:T(2,128)} %subfault_hbm.1, f32[1]{0:T(128)S(6)} %copy.13.step_hbm, s32[32]{0:T(128)} %gauge_hbm.1, f32[4,32]{1,0:T(4,128)} %misfit_hbm.1, f32[8]{0:T(128)} %source_hbm.1, f32[8]{0:T(128)} %background_hbm.1, ...), custom_call_target="tpu_custom_call" | custom-call | flops 4000000 | bytes 1100000 | tf_op jit(solution)/shard_map/adjoint/pallas_call | solution.py:492
  29.2 1.6 %hand_over.1 = (f32[2,128,128]{2,1,0:T(8,128)}, f32[8]{0:T(128)}) custom-call(f32[2,128,128]{2,1,0:T(8,128)} %get-tuple-element.4.surface, f32[8]{0:T(128)} %get-tuple-element.5.updated), custom_call_target="tpu_custom_call" | custom-call | tf_op jit(solution)/shard_map/hand_over/pallas_call | solution.py:530
